TPU v7x, 512 devices: a whole 4x8x8 slice. The times are simulated.
512 devices in a mesh: gx: 128 (over z, y, core), gy: 4 (over x).
Axes of the slice: x: 4, y: 8, z: 8, core: 2. Of those that a mesh axis runs over, the one named last changes fastest.
Arguments:
- source: float32 [64, 512, 8, 128], P(None, 'gx', 'gy'), may hold values from -6 to 6
- conductivity: float32 [512, 8, 128], P('gx', 'gy'), may hold values from 0.5 to 4
- diag_block: float32 [64, 64], replicated, as said below
- face_blocks: float32 [6, 64, 64], replicated
- smoother: float32 [64, 64], replicated
- prolong: float32 [4, 64, 64], replicated, may hold values from -0.75 to 0.75
Outputs:
- solution: float32 [64, 512, 8, 128], P(None, 'gx', 'gy')
- final_residual: float32 [64, 512, 8, 128], P(None, 'gx', 'gy')
Inputs may be any that keep to these rules, and one draw needn't show every extreme that they name: diag_block has diagonal entries between 7 and 9 and small off-diagonal entries; face_blocks have diagonal entries between 0.7 and 1 and small off-diagonal entries; smoother has diagonal entries between 0.115 and 0.135 and small off-diagonal entries.
All inputs are finite; a program needn't handle non-finite values.
Results may differ from a plain program's by a relative error of at most 0.0003.
Values sent between devices are 32-bit elements; how exact they have to be, the bound alone decides.
A program may use at most 64 MiB of HBM per device.

v0:
```python
import jax
import jax.numpy as jnp
from jax import lax
from jax.sharding import PartitionSpec as P

COARSE_SWEEPS = 3


OMEGA = 0.8


def shifted(block, axis, distance):
    devices = range(lax.axis_size(axis))
    route = [(i - distance, i) for i in devices if i - distance in devices]
    return lax.ppermute(block, axis, route)


def extended(block, sides, width):
    for axis, dim in sides:
        count = lax.axis_size(axis)
        forward = [(i, i + 1) for i in range(count - 1)]
        backward = [(target, source) for source, target in forward]
        low = lax.ppermute(
            lax.slice_in_dim(block, block.shape[dim] - width, None, axis=dim), axis, forward
        )
        high = lax.ppermute(lax.slice_in_dim(block, 0, width, axis=dim), axis, backward)
        block = jnp.concatenate([low, block, high], axis=dim)
    return block


def multiply(matrix, values):
    return jnp.tensordot(matrix, values, axes=1, precision=lax.Precision.HIGHEST)


def block_apply(padded, coefficient, blocks):
    diag_block, face_blocks, smoother = blocks
    center = padded[:, 1:-1, 1:-1]
    z_padded = jnp.pad(center, ((0, 0), (0, 0), (0, 0), (1, 1)))
    beside = (
        padded[:, :-2, 1:-1],
        padded[:, 2:, 1:-1],
        padded[:, 1:-1, :-2],
        padded[:, 1:-1, 2:],
        z_padded[:, :, :, :-2],
        z_padded[:, :, :, 2:],
    )
    total_sum = multiply(diag_block, center)
    for number in range(6):
        total_sum = total_sum - multiply(face_blocks[number], beside[number])
    return coefficient[None] * total_sum


def relax(iterate, source, coefficient, image, smoother):
    return iterate + OMEGA * multiply(smoother, (source - image) / coefficient[None])


def restrict_level(residual, coefficient, prolong):
    depth, span_x, span_y, span_z = residual.shape
    halves = residual.reshape(depth, span_x // 2, 2, span_y // 2, 2, span_z)
    tables = prolong.reshape(2, 2, depth, depth)
    coarse = 0.25 * jnp.einsum("acji,jxaycz->ixyz", tables, halves, precision=lax.Precision.HIGHEST)
    coarse_coef = jnp.mean(coefficient.reshape(span_x // 2, 2, span_y // 2, 2, span_z), axis=(1, 3))
    return (coarse, coarse_coef)


def prolong_level(coarse, prolong):
    depth, span_x, span_y, span_z = coarse.shape
    tables = prolong.reshape(2, 2, depth, depth)
    finer = jnp.einsum("acji,ixyz->jxaycz", tables, coarse, precision=lax.Precision.HIGHEST)
    return finer.reshape(depth, 2 * span_x, 2 * span_y, span_z)


def collect_group(group_source, group_coef):
    position = lax.axis_index("gx") % 4
    slots = [(jnp.zeros_like(group_source), jnp.zeros_like(group_coef)) for target in range(4)]
    for offset in (3, 2, 1, 0, -1, -2, -3):
        if offset == 0:
            received = (group_source, group_coef)
        else:
            received = shifted((group_source, group_coef), "gx", offset)
        anchor = position - offset
        for target in range(4):
            slots[target] = (
                jnp.where(anchor == target, received[0], slots[target][0]),
                jnp.where(anchor == target, received[1], slots[target][1]),
            )
    whole_source = jnp.concatenate([entry[0] for entry in slots], axis=1)
    whole_coef = jnp.concatenate([entry[1] for entry in slots], axis=0)
    return (whole_source, whole_coef)


def level_two(source, coefficient, blocks):
    smoother = blocks[2]
    iterate = OMEGA * multiply(smoother, source / coefficient[None])
    for sweep_id in range(COARSE_SWEEPS - 1):
        planes = []
        for offset in (4, -4):
            boundary = iterate[:, -1:] if offset > 0 else iterate[:, :1]
            planes.append(shifted(boundary, "gx", offset))
        padded = jnp.concatenate([planes[0], iterate, planes[1]], axis=1)
        padded = jnp.pad(padded, ((0, 0), (0, 0), (1, 1), (0, 0)))
        iterate = relax(
            iterate, source, coefficient, block_apply(padded, coefficient, blocks), smoother
        )
    return iterate


def level_one(source, coefficient, blocks, prolong, one_apply):
    smoother = blocks[2]
    iterate = OMEGA * multiply(smoother, source / coefficient[None])
    iterate = relax(iterate, source, coefficient, one_apply(iterate), smoother)
    residual = source - one_apply(iterate)
    group_source, group_coef = restrict_level(residual, coefficient, prolong)
    whole_source, whole_coef = collect_group(group_source, group_coef)
    coarse_fix = level_two(whole_source, whole_coef, blocks)
    position = lax.axis_index("gx") % 4
    span_x = group_source.shape[1]
    share = lax.dynamic_slice_in_dim(coarse_fix, position * span_x, span_x, axis=1)
    iterate = iterate + prolong_level(share, prolong)
    return relax(iterate, source, coefficient, one_apply(iterate), smoother)


def shards(source, conductivity, diag_block, face_blocks, smoother, prolong):
    blocks = (diag_block, face_blocks, smoother)

    def fine_apply(values):
        padded = extended(values, (("gx", 1), ("gy", 2)), 1)
        return block_apply(padded, conductivity, blocks)

    iterate = OMEGA * multiply(smoother, source / conductivity[None])
    padded = extended(iterate, (("gx", 1), ("gy", 2)), 1)
    iterate = relax(
        iterate, source, conductivity, block_apply(padded, conductivity, blocks), smoother
    )
    residual = source - fine_apply(iterate)
    coarse_source, coarse_coef = restrict_level(residual, conductivity, prolong)
    level_source, level_coef = (
        lax.all_gather(coarse_source, "gy", axis=2, tiled=True),
        lax.all_gather(coarse_coef, "gy", axis=1, tiled=True),
    )

    def wide_apply(values):
        padded_one = extended(values, (("gx", 1),), 1)
        padded_one = jnp.pad(padded_one, ((0, 0), (0, 0), (1, 1), (0, 0)))
        return block_apply(padded_one, level_coef, blocks)

    level_fix = level_one(level_source, level_coef, blocks, prolong, wide_apply)
    span_y = coarse_source.shape[2]
    share = lax.dynamic_slice_in_dim(level_fix, lax.axis_index("gy") * span_y, span_y, axis=2)
    iterate = iterate + prolong_level(share, prolong)
    iterate = relax(iterate, source, conductivity, fine_apply(iterate), smoother)
    final_residual = source - fine_apply(iterate)
    return (iterate, final_residual)


def solution(mesh):
    return jax.shard_map(
        shards,
        mesh=mesh,
        in_specs=(P(None, "gx", "gy", None), P("gx", "gy", None), P(), P(), P(), P()),
        out_specs=(P(None, "gx", "gy", None), P(None, "gx", "gy", None)),
        check_vma=False,
    )
```

profile of v0, /device:TPU:249, one launch (start us, length us, event | category | flops | bytes accessed | tf_op | source)
XLA Modules:
  0.0 241.5 jit_solution(17297014910098183040)
XLA Ops:
  0.6 0.7 reduce_sum.23
  1.4 7.7 %all-gather.1 = f32[2,512]{1,0:T(2,128)S(1)} all-gather(f32[2,128]{1,0:T(2,128)S(1)} %broadcast_multiply_fusion), channel_id=3, replica_groups=mesh['gx'=128,'gy'=4] {'gy'}, dimensions={1}, use_global_device_ids=true | all-gather | bytes 5120 | tf_op jit(solution)/shard_map/all_gather | solution.py:139
  9.2 5.6 %collective-permute-start.18 = (f32[1,2,128]{2,1,0:T(2,128)S(1)}, f32[1,2,128]{2,1,0:T(2,128)S(1)}, u32[]{:S(2)}, u32[]{:S(2)}) collective-permute-start(f32[1,2,128]{2,1,0:T(2,128)S(1)} %multiply_bitcast_fusion), channel_id=1, source_target_pairs={{12,0},{16,4},{20,8},{24,12},{28,16},{32,20},{36,24},{40,28},{44,3... | collective-permute-start | bytes 3080 | tf_op jit(solution)/shard_map/ppermute | solution.py:15
  14.7 3.0 %collective-permute-start.19 = (f32[1,2,128]{2,1,0:T(2,128)S(1)}, f32[1,2,128]{2,1,0:T(2,128)S(1)}, u32[]{:S(2)}, u32[]{:S(2)}) collective-permute-start(f32[1,2,128]{2,1,0:T(2,128)S(1)} %multiply_bitcast_fusion), channel_id=1, source_target_pairs={{8,0},{12,4},{16,8},{20,12},{24,16},{28,20},{32,24},{36,28},{40,32... | collective-permute-start | bytes 3080 | tf_op jit(solution)/shard_map/ppermute | solution.py:15
  17.7 1.9 collective-permute-start.20
  19.6 7.0 %collective-permute-start.21 = (f32[1,2,128]{2,1,0:T(2,128)S(1)}, f32[1,2,128]{2,1,0:T(2,128)S(1)}, u32[]{:S(2)}, u32[]{:S(2)}) collective-permute-start(f32[1,2,128]{2,1,0:T(2,128)S(1)} %multiply_bitcast_fusion), channel_id=1, source_target_pairs={{0,4},{4,8},{8,12},{12,16},{16,20},{20,24},{24,28},{28,32},{32,36}... | collective-permute-start | bytes 3080 | tf_op jit(solution)/shard_map/ppermute | solution.py:15
  26.6 2.3 collective-permute-start.22
  29.0 0.7 copy-done.5
  29.7 1.3 fusion.48
  31.0 0.7 copy-done.2
  33.2 2.3 collective-permute-start.23
  35.6 2.2 collective-permute-start
  37.8 2.1 collective-permute-start.1
  40.0 6.7 %collective-permute-done.1 = f32[64,1,2,128]{3,0,2,1:T(8,128)S(1)} collective-permute-done((f32[64,1,2,128]{3,0,2,1:T(8,128)S(1)}, f32[64,1,2,128]{3,0,2,1:T(8,128)S(1)}, u32[]{:S(2)}, u32[]{:S(2)}) %collective-permute-start.1) | collective-permute-done | bytes 65568 | tf_op jit(solution)/shard_map/ppermute | solution.py:26
  46.8 1.3 collective-permute-start.2
  48.1 1.3 collective-permute-start.3
  49.8 0.9 collective-permute-done.2
  51.0 3.5 %collective-permute-done.3 = f32[64,6,1,128]{3,0,2,1:T(8,128)S(1)} collective-permute-done((f32[64,6,1,128]{3,0,2,1:T(8,128)S(1)}, f32[64,6,1,128]{3,0,2,1:T(8,128)S(1)}, u32[]{:S(2)}, u32[]{:S(2)}) %collective-permute-start.3) | collective-permute-done | bytes 196640 | tf_op jit(solution)/shard_map/ppermute | solution.py:26
  57.1 3.2 %collective-permute-start.4 = (f32[64,1,2,128]{3,0,2,1:T(8,128)S(1)}, f32[64,1,2,128]{3,0,2,1:T(8,128)S(1)}, u32[]{:S(2)}, u32[]{:S(2)}) collective-permute-start(f32[64,1,2,128]{3,0,2,1:T(8,128)S(1)} %get-tuple-element.28), channel_id=1, source_target_pairs={{0,4},{4,8},{8,12},{12,16},{16,20},{20,24},{24,28},{28,32},{32,36}... | collective-permute-start | bytes 196616 | tf_op jit(solution)/shard_map/ppermute | solution.py:23
  60.4 1.9 collective-permute-start.5
  62.8 6.5 %collective-permute-done.5 = f32[64,1,2,128]{3,0,2,1:T(8,128)S(1)} collective-permute-done((f32[64,1,2,128]{3,0,2,1:T(8,128)S(1)}, f32[64,1,2,128]{3,0,2,1:T(8,128)S(1)}, u32[]{:S(2)}, u32[]{:S(2)}) %collective-permute-start.5) | collective-permute-done | bytes 65568 | tf_op jit(solution)/shard_map/ppermute | solution.py:26
  69.4 2.8 %collective-permute-start.6 = (f32[64,6,1,128]{3,0,2,1:T(8,128)S(1)}, f32[64,6,1,128]{3,0,2,1:T(8,128)S(1)}, u32[]{:S(2)}, u32[]{:S(2)}) collective-permute-start(f32[64,6,1,128]{3,0,2,1:T(8,128)S(1)} %get-tuple-element.10), channel_id=1, source_target_pairs={{0,1},{1,2},{2,3},{4,5},{5,6},{6,7},{8,9},{9,10},{10,11},{12,13},{... | collective-permute-start | bytes 589832 | tf_op jit(solution)/shard_map/ppermute | solution.py:23
  72.2 1.3 collective-permute-start.7
  73.9 0.9 collective-permute-done.6
  75.1 3.5 %collective-permute-done.7 = f32[64,6,1,128]{3,0,2,1:T(8,128)S(1)} collective-permute-done((f32[64,6,1,128]{3,0,2,1:T(8,128)S(1)}, f32[64,6,1,128]{3,0,2,1:T(8,128)S(1)}, u32[]{:S(2)}, u32[]{:S(2)}) %collective-permute-start.7) | collective-permute-done | bytes 196640 | tf_op jit(solution)/shard_map/ppermute | solution.py:26
  80.3 9.4 %all-gather = f32[64,2,512]{2,0,1:T(8,128)S(1)} all-gather(f32[64,2,128]{2,0,1:T(8,128)S(1)} %fusion.74), channel_id=2, replica_groups=mesh['gx'=128,'gy'=4] {'gy'}, dimensions={2}, use_global_device_ids=true | all-gather | bytes 327680 | tf_op jit(solution)/shard_map/all_gather | solution.py:138
  90.5 6.4 %collective-permute-start.8 = (f32[64,1,4,128]{3,0,2,1:T(8,128)S(1)}, f32[64,1,4,128]{3,0,2,1:T(8,128)S(1)}, u32[]{:S(2)}, u32[]{:S(2)}) collective-permute-start(f32[64,1,4,128]{3,0,2,1:T(8,128)S(1)} %get-tuple-element.26), channel_id=1, source_target_pairs={{0,4},{4,8},{8,12},{12,16},{16,20},{20,24},{24,28},{28,32},{32,36}... | collective-permute-start | bytes 393224 | tf_op jit(solution)/shard_map/ppermute | solution.py:23
  96.9 1.9 collective-permute-start.9
  99.3 7.2 %collective-permute-done.9 = f32[64,1,4,128]{3,0,2,1:T(8,128)S(1)} collective-permute-done((f32[64,1,4,128]{3,0,2,1:T(8,128)S(1)}, f32[64,1,4,128]{3,0,2,1:T(8,128)S(1)}, u32[]{:S(2)}, u32[]{:S(2)}) %collective-permute-start.9) | collective-permute-done | bytes 131104 | tf_op jit(solution)/shard_map/ppermute | solution.py:26
  109.3 1.9 collective-permute-start.10
  111.2 2.6 %collective-permute-start.11 = (f32[64,1,4,128]{3,0,2,1:T(8,128)S(1)}, f32[64,1,4,128]{3,0,2,1:T(8,128)S(1)}, u32[]{:S(2)}, u32[]{:S(2)}) collective-permute-start(f32[64,1,4,128]{3,0,2,1:T(8,128)S(1)} %get-tuple-element.25), channel_id=1, source_target_pairs={{4,0},{8,4},{12,8},{16,12},{20,16},{24,20},{28,24},{32,28},{36,32}... | collective-permute-start | bytes 393224 | tf_op jit(solution)/shard_map/ppermute | solution.py:26
  114.3 6.5 %collective-permute-done.11 = f32[64,1,4,128]{3,0,2,1:T(8,128)S(1)} collective-permute-done((f32[64,1,4,128]{3,0,2,1:T(8,128)S(1)}, f32[64,1,4,128]{3,0,2,1:T(8,128)S(1)}, u32[]{:S(2)}, u32[]{:S(2)}) %collective-permute-start.11) | collective-permute-done | bytes 131104 | tf_op jit(solution)/shard_map/ppermute | solution.py:26
  123.2 1.9 collective-permute-start.12
  125.1 1.9 collective-permute-start.13
  127.0 1.9 collective-permute-start.14
  129.0 7.0 %collective-permute-start.15 = (f32[64,1,2,128]{3,0,2,1:T(8,128)S(1)}, f32[64,1,2,128]{3,0,2,1:T(8,128)S(1)}, u32[]{:S(2)}, u32[]{:S(2)}) collective-permute-start(f32[64,1,2,128]{3,0,2,1:T(8,128)S(1)} %fusion.76), channel_id=1, source_target_pairs={{0,4},{4,8},{8,12},{12,16},{16,20},{20,24},{24,28},{28,32},{32,36}... | collective-permute-start | bytes 196616 | tf_op jit(solution)/shard_map/ppermute | solution.py:15
  135.9 3.4 %collective-permute-start.16 = (f32[64,1,2,128]{3,0,2,1:T(8,128)S(1)}, f32[64,1,2,128]{3,0,2,1:T(8,128)S(1)}, u32[]{:S(2)}, u32[]{:S(2)}) collective-permute-start(f32[64,1,2,128]{3,0,2,1:T(8,128)S(1)} %fusion.76), channel_id=1, source_target_pairs={{0,8},{4,12},{8,16},{12,20},{16,24},{20,28},{24,32},{28,36},{32,40... | collective-permute-start | bytes 196616 | tf_op jit(solution)/shard_map/ppermute | solution.py:15
  139.3 3.9 %collective-permute-start.17 = (f32[64,1,2,128]{3,0,2,1:T(8,128)S(1)}, f32[64,1,2,128]{3,0,2,1:T(8,128)S(1)}, u32[]{:S(2)}, u32[]{:S(2)}) collective-permute-start(f32[64,1,2,128]{3,0,2,1:T(8,128)S(1)} %fusion.76), channel_id=1, source_target_pairs={{0,12},{4,16},{8,20},{12,24},{16,28},{20,32},{24,36},{28,40},{32,4... | collective-permute-start | bytes 196616 | tf_op jit(solution)/shard_map/ppermute | solution.py:15
  143.2 2.3 collective-permute-done.17
  146.5 2.8 %collective-permute-start.24 = (f32[64,1,2,128]{3,0,2,1:T(8,128)S(1)}, f32[64,1,2,128]{3,0,2,1:T(8,128)S(1)}, u32[]{:S(2)}, u32[]{:S(2)}) collective-permute-start(f32[64,1,2,128]{3,0,2,1:T(8,128)S(1)} %get-tuple-element.22), channel_id=1, source_target_pairs={{0,16},{4,20},{8,24},{12,28},{16,32},{20,36},{24,40},{28,44},{32,4... | collective-permute-start | bytes 196616 | tf_op jit(solution)/shard_map/ppermute | solution.py:15
  149.3 3.4 %collective-permute-start.25 = (f32[64,1,2,128]{3,0,2,1:T(8,128)S(1)}, f32[64,1,2,128]{3,0,2,1:T(8,128)S(1)}, u32[]{:S(2)}, u32[]{:S(2)}) collective-permute-start(f32[64,1,2,128]{3,0,2,1:T(8,128)S(1)} %get-tuple-element.23), channel_id=1, source_target_pairs={{16,0},{20,4},{24,8},{28,12},{32,16},{36,20},{40,24},{44,28},{48,3... | collective-permute-start | bytes 196616 | tf_op jit(solution)/shard_map/ppermute | solution.py:15
  153.5 5.1 %collective-permute-done.25 = f32[64,1,2,128]{3,0,2,1:T(8,128)S(1)} collective-permute-done((f32[64,1,2,128]{3,0,2,1:T(8,128)S(1)}, f32[64,1,2,128]{3,0,2,1:T(8,128)S(1)}, u32[]{:S(2)}, u32[]{:S(2)}) %collective-permute-start.25) | collective-permute-done | bytes 65568 | tf_op jit(solution)/shard_map/ppermute | solution.py:15
  161.3 1.9 collective-permute-start.26
  163.2 4.3 %collective-permute-start.27 = (f32[64,1,2,128]{3,0,2,1:T(8,128)S(1)}, f32[64,1,2,128]{3,0,2,1:T(8,128)S(1)}, u32[]{:S(2)}, u32[]{:S(2)}) collective-permute-start(f32[64,1,2,128]{3,0,2,1:T(8,128)S(1)} %get-tuple-element.21), channel_id=1, source_target_pairs={{16,0},{20,4},{24,8},{28,12},{32,16},{36,20},{40,24},{44,28},{48,3... | collective-permute-start | bytes 196616 | tf_op jit(solution)/shard_map/ppermute | solution.py:15
  167.9 5.2 %collective-permute-done.27 = f32[64,1,2,128]{3,0,2,1:T(8,128)S(1)} collective-permute-done((f32[64,1,2,128]{3,0,2,1:T(8,128)S(1)}, f32[64,1,2,128]{3,0,2,1:T(8,128)S(1)}, u32[]{:S(2)}, u32[]{:S(2)}) %collective-permute-start.27) | collective-permute-done | bytes 65568 | tf_op jit(solution)/shard_map/ppermute | solution.py:15
  176.3 7.4 %collective-permute-start.28 = (f32[64,1,4,128]{3,0,2,1:T(8,128)S(1)}, f32[64,1,4,128]{3,0,2,1:T(8,128)S(1)}, u32[]{:S(2)}, u32[]{:S(2)}) collective-permute-start(f32[64,1,4,128]{3,0,2,1:T(8,128)S(1)} %get-tuple-element.18), channel_id=1, source_target_pairs={{0,4},{4,8},{8,12},{12,16},{16,20},{20,24},{24,28},{28,32},{32,36}... | collective-permute-start | bytes 393224 | tf_op jit(solution)/shard_map/ppermute | solution.py:23
  183.7 4.4 %collective-permute-start.29 = (f32[64,1,4,128]{3,0,2,1:T(8,128)S(1)}, f32[64,1,4,128]{3,0,2,1:T(8,128)S(1)}, u32[]{:S(2)}, u32[]{:S(2)}) collective-permute-start(f32[64,1,4,128]{3,0,2,1:T(8,128)S(1)} %get-tuple-element.19), channel_id=1, source_target_pairs={{4,0},{8,4},{12,8},{16,12},{20,16},{24,20},{28,24},{32,28},{36,32}... | collective-permute-start | bytes 393224 | tf_op jit(solution)/shard_map/ppermute | solution.py:26
  188.6 4.8 %collective-permute-done.29 = f32[64,1,4,128]{3,0,2,1:T(8,128)S(1)} collective-permute-done((f32[64,1,4,128]{3,0,2,1:T(8,128)S(1)}, f32[64,1,4,128]{3,0,2,1:T(8,128)S(1)}, u32[]{:S(2)}, u32[]{:S(2)}) %collective-permute-start.29) | collective-permute-done | bytes 131104 | tf_op jit(solution)/shard_map/ppermute | solution.py:26
  196.5 1.9 collective-permute-start.30
  198.4 2.4 collective-permute-start.31
  201.3 6.0 %collective-permute-done.31 = f32[64,1,2,128]{3,0,2,1:T(8,128)S(1)} collective-permute-done((f32[64,1,2,128]{3,0,2,1:T(8,128)S(1)}, f32[64,1,2,128]{3,0,2,1:T(8,128)S(1)}, u32[]{:S(2)}, u32[]{:S(2)}) %collective-permute-start.31) | collective-permute-done | bytes 65568 | tf_op jit(solution)/shard_map/ppermute | solution.py:26
  207.4 1.3 collective-permute-start.32
  208.7 1.3 collective-permute-start.33
  210.4 0.9 collective-permute-done.32
  211.7 3.5 %collective-permute-done.33 = f32[64,6,1,128]{3,0,2,1:T(8,128)S(1)} collective-permute-done((f32[64,6,1,128]{3,0,2,1:T(8,128)S(1)}, f32[64,6,1,128]{3,0,2,1:T(8,128)S(1)}, u32[]{:S(2)}, u32[]{:S(2)}) %collective-permute-start.33) | collective-permute-done | bytes 196640 | tf_op jit(solution)/shard_map/ppermute | solution.py:26
  217.2 3.0 %collective-permute-start.34 = (f32[64,1,2,128]{3,0,2,1:T(8,128)S(1)}, f32[64,1,2,128]{3,0,2,1:T(8,128)S(1)}, u32[]{:S(2)}, u32[]{:S(2)}) collective-permute-start(f32[64,1,2,128]{3,0,2,1:T(8,128)S(1)} %get-tuple-element.14), channel_id=1, source_target_pairs={{0,4},{4,8},{8,12},{12,16},{16,20},{20,24},{24,28},{28,32},{32,36}... | collective-permute-start | bytes 196616 | tf_op jit(solution)/shard_map/ppermute | solution.py:23
  220.3 1.9 collective-permute-start.35
  222.7 0.9 copy.36
  223.6 5.6 %collective-permute-done.35 = f32[64,1,2,128]{3,0,2,1:T(8,128)S(1)} collective-permute-done((f32[64,1,2,128]{3,0,2,1:T(8,128)S(1)}, f32[64,1,2,128]{3,0,2,1:T(8,128)S(1)}, u32[]{:S(2)}, u32[]{:S(2)}) %collective-permute-start.35) | collective-permute-done | bytes 65568 | tf_op jit(solution)/shard_map/ppermute | solution.py:26
  229.2 3.6 %collective-permute-start.36 = (f32[64,6,1,128]{3,0,2,1:T(8,128)S(1)}, f32[64,6,1,128]{3,0,2,1:T(8,128)S(1)}, u32[]{:S(2)}, u32[]{:S(2)}) collective-permute-start(f32[64,6,1,128]{3,0,2,1:T(8,128)S(1)} %get-tuple-element.6), channel_id=1, source_target_pairs={{0,1},{1,2},{2,3},{4,5},{5,6},{6,7},{8,9},{9,10},{10,11},{12,13},{... | collective-permute-start | bytes 589832 | tf_op jit(solution)/shard_map/ppermute | solution.py:23
  232.9 1.3 collective-permute-start.37
  234.6 0.9 collective-permute-done.36
  235.8 3.5 %collective-permute-done.37 = f32[64,6,1,128]{3,0,2,1:T(8,128)S(1)} collective-permute-done((f32[64,6,1,128]{3,0,2,1:T(8,128)S(1)}, f32[64,6,1,128]{3,0,2,1:T(8,128)S(1)}, u32[]{:S(2)}, u32[]{:S(2)}) %collective-permute-start.37) | collective-permute-done | bytes 196640 | tf_op jit(solution)/shard_map/ppermute | solution.py:26
  240.6 0.9 copy.37
  (140 shorter events, 32.0 us)
Async XLA Ops:
  0.6 79.3 %copy-start = (f32[4,64,64]{2,1,0:T(8,128)S(1)}, f32[4,64,64]{2,1,0:T(8,128)}, u32[]{:S(2)}) copy-start(f32[4,64,64]{2,1,0:T(8,128)} %param.11) | copy-start | bytes 196612
  9.2 19.8 %copy-start.3 = (f32[64,64]{1,0:T(8,128)S(1)}, f32[64,64]{1,0:T(8,128)}, u32[]{:S(2)}) copy-start(f32[64,64]{1,0:T(8,128)} %param.10) | copy-start | bytes 49156
  9.2 24.1 %collective-permute-start.18 = (f32[1,2,128]{2,1,0:T(2,128)S(1)}, f32[1,2,128]{2,1,0:T(2,128)S(1)}, u32[]{:S(2)}, u32[]{:S(2)}) collective-permute-start(f32[1,2,128]{2,1,0:T(2,128)S(1)} %multiply_bitcast_fusion), channel_id=1, source_target_pairs={{12,0},{16,4},{20,8},{24,12},{28,16},{32,20},{36,24},{40,28},{44,3... | collective-permute-start | bytes 3080 | tf_op jit(solution)/shard_map/ppermute | solution.py:15
  14.7 20.9 %collective-permute-start.19 = (f32[1,2,128]{2,1,0:T(2,128)S(1)}, f32[1,2,128]{2,1,0:T(2,128)S(1)}, u32[]{:S(2)}, u32[]{:S(2)}) collective-permute-start(f32[1,2,128]{2,1,0:T(2,128)S(1)} %multiply_bitcast_fusion), channel_id=1, source_target_pairs={{8,0},{12,4},{16,8},{20,12},{24,16},{28,20},{32,24},{36,28},{40,32... | collective-permute-start | bytes 3080 | tf_op jit(solution)/shard_map/ppermute | solution.py:15
  17.7 20.1 %collective-permute-start.20 = (f32[1,2,128]{2,1,0:T(2,128)S(1)}, f32[1,2,128]{2,1,0:T(2,128)S(1)}, u32[]{:S(2)}, u32[]{:S(2)}) collective-permute-start(f32[1,2,128]{2,1,0:T(2,128)S(1)} %multiply_bitcast_fusion), channel_id=1, source_target_pairs={{4,0},{8,4},{12,8},{16,12},{20,16},{24,20},{28,24},{32,28},{36,32}... | collective-permute-start | bytes 3080 | tf_op jit(solution)/shard_map/ppermute | solution.py:15
  19.6 20.3 %collective-permute-start.21 = (f32[1,2,128]{2,1,0:T(2,128)S(1)}, f32[1,2,128]{2,1,0:T(2,128)S(1)}, u32[]{:S(2)}, u32[]{:S(2)}) collective-permute-start(f32[1,2,128]{2,1,0:T(2,128)S(1)} %multiply_bitcast_fusion), channel_id=1, source_target_pairs={{0,4},{4,8},{8,12},{12,16},{16,20},{20,24},{24,28},{28,32},{32,36}... | collective-permute-start | bytes 3080 | tf_op jit(solution)/shard_map/ppermute | solution.py:15
  26.6 13.3 %collective-permute-start.22 = (f32[1,2,128]{2,1,0:T(2,128)S(1)}, f32[1,2,128]{2,1,0:T(2,128)S(1)}, u32[]{:S(2)}, u32[]{:S(2)}) collective-permute-start(f32[1,2,128]{2,1,0:T(2,128)S(1)} %multiply_bitcast_fusion), channel_id=1, source_target_pairs={{0,8},{4,12},{8,16},{12,20},{16,24},{20,28},{24,32},{28,36},{32,40... | collective-permute-start | bytes 3080 | tf_op jit(solution)/shard_map/ppermute | solution.py:15
  29.0 0.7 copy-start.5
  31.0 0.8 copy-start.2
  31.8 0.9 copy-start.1
  33.2 6.7 %collective-permute-start.23 = (f32[1,2,128]{2,1,0:T(2,128)S(1)}, f32[1,2,128]{2,1,0:T(2,128)S(1)}, u32[]{:S(2)}, u32[]{:S(2)}) collective-permute-start(f32[1,2,128]{2,1,0:T(2,128)S(1)} %multiply_bitcast_fusion), channel_id=1, source_target_pairs={{0,12},{4,16},{8,20},{12,24},{16,28},{20,32},{24,36},{28,40},{32,4... | collective-permute-start | bytes 3080 | tf_op jit(solution)/shard_map/ppermute | solution.py:15
  35.6 4.4 %collective-permute-start = (f32[64,1,2,128]{3,0,2,1:T(8,128)S(1)}, f32[64,1,2,128]{3,0,2,1:T(8,128)S(1)}, u32[]{:S(2)}, u32[]{:S(2)}) collective-permute-start(f32[64,1,2,128]{3,0,2,1:T(8,128)S(1)} %get-tuple-element.30), channel_id=1, source_target_pairs={{0,4},{4,8},{8,12},{12,16},{16,20},{20,24},{24,28},{28,32},{32,36}... | collective-permute-start | bytes 196616 | tf_op jit(solution)/shard_map/ppermute | solution.py:23
  37.8 8.9 %collective-permute-start.1 = (f32[64,1,2,128]{3,0,2,1:T(8,128)S(1)}, f32[64,1,2,128]{3,0,2,1:T(8,128)S(1)}, u32[]{:S(2)}, u32[]{:S(2)}) collective-permute-start(f32[64,1,2,128]{3,0,2,1:T(8,128)S(1)} %get-tuple-element.31), channel_id=1, source_target_pairs={{4,0},{8,4},{12,8},{16,12},{20,16},{24,20},{28,24},{32,28},{36,32}... | collective-permute-start | bytes 196616 | tf_op jit(solution)/shard_map/ppermute | solution.py:26
  46.8 3.9 %collective-permute-start.2 = (f32[64,6,1,128]{3,0,2,1:T(8,128)S(1)}, f32[64,6,1,128]{3,0,2,1:T(8,128)S(1)}, u32[]{:S(2)}, u32[]{:S(2)}) collective-permute-start(f32[64,6,1,128]{3,0,2,1:T(8,128)S(1)} %get-tuple-element.12), channel_id=1, source_target_pairs={{0,1},{1,2},{2,3},{4,5},{5,6},{6,7},{8,9},{9,10},{10,11},{12,13},{... | collective-permute-start | bytes 589832 | tf_op jit(solution)/shard_map/ppermute | solution.py:23
  48.1 6.4 %collective-permute-start.3 = (f32[64,6,1,128]{3,0,2,1:T(8,128)S(1)}, f32[64,6,1,128]{3,0,2,1:T(8,128)S(1)}, u32[]{:S(2)}, u32[]{:S(2)}) collective-permute-start(f32[64,6,1,128]{3,0,2,1:T(8,128)S(1)} %get-tuple-element.13), channel_id=1, source_target_pairs={{1,0},{2,1},{3,2},{5,4},{6,5},{7,6},{9,8},{10,9},{11,10},{13,12},{... | collective-permute-start | bytes 589832 | tf_op jit(solution)/shard_map/ppermute | solution.py:26
  54.9 1.0 copy-start.4
  57.1 5.7 %collective-permute-start.4 = (f32[64,1,2,128]{3,0,2,1:T(8,128)S(1)}, f32[64,1,2,128]{3,0,2,1:T(8,128)S(1)}, u32[]{:S(2)}, u32[]{:S(2)}) collective-permute-start(f32[64,1,2,128]{3,0,2,1:T(8,128)S(1)} %get-tuple-element.28), channel_id=1, source_target_pairs={{0,4},{4,8},{8,12},{12,16},{16,20},{20,24},{24,28},{28,32},{32,36}... | collective-permute-start | bytes 196616 | tf_op jit(solution)/shard_map/ppermute | solution.py:23
  60.4 8.9 %collective-permute-start.5 = (f32[64,1,2,128]{3,0,2,1:T(8,128)S(1)}, f32[64,1,2,128]{3,0,2,1:T(8,128)S(1)}, u32[]{:S(2)}, u32[]{:S(2)}) collective-permute-start(f32[64,1,2,128]{3,0,2,1:T(8,128)S(1)} %get-tuple-element.29), channel_id=1, source_target_pairs={{4,0},{8,4},{12,8},{16,12},{20,16},{24,20},{28,24},{32,28},{36,32}... | collective-permute-start | bytes 196616 | tf_op jit(solution)/shard_map/ppermute | solution.py:26
  69.4 5.4 %collective-permute-start.6 = (f32[64,6,1,128]{3,0,2,1:T(8,128)S(1)}, f32[64,6,1,128]{3,0,2,1:T(8,128)S(1)}, u32[]{:S(2)}, u32[]{:S(2)}) collective-permute-start(f32[64,6,1,128]{3,0,2,1:T(8,128)S(1)} %get-tuple-element.10), channel_id=1, source_target_pairs={{0,1},{1,2},{2,3},{4,5},{5,6},{6,7},{8,9},{9,10},{10,11},{12,13},{... | collective-permute-start | bytes 589832 | tf_op jit(solution)/shard_map/ppermute | solution.py:23
  72.2 6.4 %collective-permute-start.7 = (f32[64,6,1,128]{3,0,2,1:T(8,128)S(1)}, f32[64,6,1,128]{3,0,2,1:T(8,128)S(1)}, u32[]{:S(2)}, u32[]{:S(2)}) collective-permute-start(f32[64,6,1,128]{3,0,2,1:T(8,128)S(1)} %get-tuple-element.11), channel_id=1, source_target_pairs={{1,0},{2,1},{3,2},{5,4},{6,5},{7,6},{9,8},{10,9},{11,10},{13,12},{... | collective-permute-start | bytes 589832 | tf_op jit(solution)/shard_map/ppermute | solution.py:26
  90.5 8.8 %collective-permute-start.8 = (f32[64,1,4,128]{3,0,2,1:T(8,128)S(1)}, f32[64,1,4,128]{3,0,2,1:T(8,128)S(1)}, u32[]{:S(2)}, u32[]{:S(2)}) collective-permute-start(f32[64,1,4,128]{3,0,2,1:T(8,128)S(1)} %get-tuple-element.26), channel_id=1, source_target_pairs={{0,4},{4,8},{8,12},{12,16},{16,20},{20,24},{24,28},{28,32},{32,36}... | collective-permute-start | bytes 393224 | tf_op jit(solution)/shard_map/ppermute | solution.py:23
  96.9 9.6 %collective-permute-start.9 = (f32[64,1,4,128]{3,0,2,1:T(8,128)S(1)}, f32[64,1,4,128]{3,0,2,1:T(8,128)S(1)}, u32[]{:S(2)}, u32[]{:S(2)}) collective-permute-start(f32[64,1,4,128]{3,0,2,1:T(8,128)S(1)} %get-tuple-element.27), channel_id=1, source_target_pairs={{4,0},{8,4},{12,8},{16,12},{20,16},{24,20},{28,24},{32,28},{36,32}... | collective-permute-start | bytes 393224 | tf_op jit(solution)/shard_map/ppermute | solution.py:26
  109.3 5.0 %collective-permute-start.10 = (f32[64,1,4,128]{3,0,2,1:T(8,128)S(1)}, f32[64,1,4,128]{3,0,2,1:T(8,128)S(1)}, u32[]{:S(2)}, u32[]{:S(2)}) collective-permute-start(f32[64,1,4,128]{3,0,2,1:T(8,128)S(1)} %get-tuple-element.24), channel_id=1, source_target_pairs={{0,4},{4,8},{8,12},{12,16},{16,20},{20,24},{24,28},{28,32},{32,36}... | collective-permute-start | bytes 393224 | tf_op jit(solution)/shard_map/ppermute | solution.py:23
  111.2 9.6 %collective-permute-start.11 = (f32[64,1,4,128]{3,0,2,1:T(8,128)S(1)}, f32[64,1,4,128]{3,0,2,1:T(8,128)S(1)}, u32[]{:S(2)}, u32[]{:S(2)}) collective-permute-start(f32[64,1,4,128]{3,0,2,1:T(8,128)S(1)} %get-tuple-element.25), channel_id=1, source_target_pairs={{4,0},{8,4},{12,8},{16,12},{20,16},{24,20},{28,24},{32,28},{36,32}... | collective-permute-start | bytes 393224 | tf_op jit(solution)/shard_map/ppermute | solution.py:26
  123.2 16.1 %collective-permute-start.12 = (f32[64,1,2,128]{3,0,2,1:T(8,128)S(1)}, f32[64,1,2,128]{3,0,2,1:T(8,128)S(1)}, u32[]{:S(2)}, u32[]{:S(2)}) collective-permute-start(f32[64,1,2,128]{3,0,2,1:T(8,128)S(1)} %fusion.76), channel_id=1, source_target_pairs={{12,0},{16,4},{20,8},{24,12},{28,16},{32,20},{36,24},{40,28},{44,3... | collective-permute-start | bytes 196616 | tf_op jit(solution)/shard_map/ppermute | solution.py:15
  125.1 18.1 %collective-permute-start.13 = (f32[64,1,2,128]{3,0,2,1:T(8,128)S(1)}, f32[64,1,2,128]{3,0,2,1:T(8,128)S(1)}, u32[]{:S(2)}, u32[]{:S(2)}) collective-permute-start(f32[64,1,2,128]{3,0,2,1:T(8,128)S(1)} %fusion.76), channel_id=1, source_target_pairs={{8,0},{12,4},{16,8},{20,12},{24,16},{28,20},{32,24},{36,28},{40,32... | collective-permute-start | bytes 196616 | tf_op jit(solution)/shard_map/ppermute | solution.py:15
  127.0 16.2 %collective-permute-start.14 = (f32[64,1,2,128]{3,0,2,1:T(8,128)S(1)}, f32[64,1,2,128]{3,0,2,1:T(8,128)S(1)}, u32[]{:S(2)}, u32[]{:S(2)}) collective-permute-start(f32[64,1,2,128]{3,0,2,1:T(8,128)S(1)} %fusion.76), channel_id=1, source_target_pairs={{4,0},{8,4},{12,8},{16,12},{20,16},{24,20},{28,24},{32,28},{36,32}... | collective-permute-start | bytes 196616 | tf_op jit(solution)/shard_map/ppermute | solution.py:15
  129.0 14.3 %collective-permute-start.15 = (f32[64,1,2,128]{3,0,2,1:T(8,128)S(1)}, f32[64,1,2,128]{3,0,2,1:T(8,128)S(1)}, u32[]{:S(2)}, u32[]{:S(2)}) collective-permute-start(f32[64,1,2,128]{3,0,2,1:T(8,128)S(1)} %fusion.76), channel_id=1, source_target_pairs={{0,4},{4,8},{8,12},{12,16},{16,20},{20,24},{24,28},{28,32},{32,36}... | collective-permute-start | bytes 196616 | tf_op jit(solution)/shard_map/ppermute | solution.py:15
  135.9 7.3 %collective-permute-start.16 = (f32[64,1,2,128]{3,0,2,1:T(8,128)S(1)}, f32[64,1,2,128]{3,0,2,1:T(8,128)S(1)}, u32[]{:S(2)}, u32[]{:S(2)}) collective-permute-start(f32[64,1,2,128]{3,0,2,1:T(8,128)S(1)} %fusion.76), channel_id=1, source_target_pairs={{0,8},{4,12},{8,16},{12,20},{16,24},{20,28},{24,32},{28,36},{32,40... | collective-permute-start | bytes 196616 | tf_op jit(solution)/shard_map/ppermute | solution.py:15
  139.3 6.3 %collective-permute-start.17 = (f32[64,1,2,128]{3,0,2,1:T(8,128)S(1)}, f32[64,1,2,128]{3,0,2,1:T(8,128)S(1)}, u32[]{:S(2)}, u32[]{:S(2)}) collective-permute-start(f32[64,1,2,128]{3,0,2,1:T(8,128)S(1)} %fusion.76), channel_id=1, source_target_pairs={{0,12},{4,16},{8,20},{12,24},{16,28},{20,32},{24,36},{28,40},{32,4... | collective-permute-start | bytes 196616 | tf_op jit(solution)/shard_map/ppermute | solution.py:15
  146.5 7.0 %collective-permute-start.24 = (f32[64,1,2,128]{3,0,2,1:T(8,128)S(1)}, f32[64,1,2,128]{3,0,2,1:T(8,128)S(1)}, u32[]{:S(2)}, u32[]{:S(2)}) collective-permute-start(f32[64,1,2,128]{3,0,2,1:T(8,128)S(1)} %get-tuple-element.22), channel_id=1, source_target_pairs={{0,16},{4,20},{8,24},{12,28},{16,32},{20,36},{24,40},{28,44},{32,4... | collective-permute-start | bytes 196616 | tf_op jit(solution)/shard_map/ppermute | solution.py:15
  149.3 9.2 %collective-permute-start.25 = (f32[64,1,2,128]{3,0,2,1:T(8,128)S(1)}, f32[64,1,2,128]{3,0,2,1:T(8,128)S(1)}, u32[]{:S(2)}, u32[]{:S(2)}) collective-permute-start(f32[64,1,2,128]{3,0,2,1:T(8,128)S(1)} %get-tuple-element.23), channel_id=1, source_target_pairs={{16,0},{20,4},{24,8},{28,12},{32,16},{36,20},{40,24},{44,28},{48,3... | collective-permute-start | bytes 196616 | tf_op jit(solution)/shard_map/ppermute | solution.py:15
  161.3 6.7 %collective-permute-start.26 = (f32[64,1,2,128]{3,0,2,1:T(8,128)S(1)}, f32[64,1,2,128]{3,0,2,1:T(8,128)S(1)}, u32[]{:S(2)}, u32[]{:S(2)}) collective-permute-start(f32[64,1,2,128]{3,0,2,1:T(8,128)S(1)} %get-tuple-element.20), channel_id=1, source_target_pairs={{0,16},{4,20},{8,24},{12,28},{16,32},{20,36},{24,40},{28,44},{32,4... | collective-permute-start | bytes 196616 | tf_op jit(solution)/shard_map/ppermute | solution.py:15
  163.2 9.9 %collective-permute-start.27 = (f32[64,1,2,128]{3,0,2,1:T(8,128)S(1)}, f32[64,1,2,128]{3,0,2,1:T(8,128)S(1)}, u32[]{:S(2)}, u32[]{:S(2)}) collective-permute-start(f32[64,1,2,128]{3,0,2,1:T(8,128)S(1)} %get-tuple-element.21), channel_id=1, source_target_pairs={{16,0},{20,4},{24,8},{28,12},{32,16},{36,20},{40,24},{44,28},{48,3... | collective-permute-start | bytes 196616 | tf_op jit(solution)/shard_map/ppermute | solution.py:15
  176.3 12.3 %collective-permute-start.28 = (f32[64,1,4,128]{3,0,2,1:T(8,128)S(1)}, f32[64,1,4,128]{3,0,2,1:T(8,128)S(1)}, u32[]{:S(2)}, u32[]{:S(2)}) collective-permute-start(f32[64,1,4,128]{3,0,2,1:T(8,128)S(1)} %get-tuple-element.18), channel_id=1, source_target_pairs={{0,4},{4,8},{8,12},{12,16},{16,20},{20,24},{24,28},{28,32},{32,36}... | collective-permute-start | bytes 393224 | tf_op jit(solution)/shard_map/ppermute | solution.py:23
  183.7 9.6 %collective-permute-start.29 = (f32[64,1,4,128]{3,0,2,1:T(8,128)S(1)}, f32[64,1,4,128]{3,0,2,1:T(8,128)S(1)}, u32[]{:S(2)}, u32[]{:S(2)}) collective-permute-start(f32[64,1,4,128]{3,0,2,1:T(8,128)S(1)} %get-tuple-element.19), channel_id=1, source_target_pairs={{4,0},{8,4},{12,8},{16,12},{20,16},{24,20},{28,24},{32,28},{36,32}... | collective-permute-start | bytes 393224 | tf_op jit(solution)/shard_map/ppermute | solution.py:26
  196.5 4.8 %collective-permute-start.30 = (f32[64,1,2,128]{3,0,2,1:T(8,128)S(1)}, f32[64,1,2,128]{3,0,2,1:T(8,128)S(1)}, u32[]{:S(2)}, u32[]{:S(2)}) collective-permute-start(f32[64,1,2,128]{3,0,2,1:T(8,128)S(1)} %get-tuple-element.16), channel_id=1, source_target_pairs={{0,4},{4,8},{8,12},{12,16},{16,20},{20,24},{24,28},{28,32},{32,36}... | collective-permute-start | bytes 196616 | tf_op jit(solution)/shard_map/ppermute | solution.py:23
  198.4 8.9 %collective-permute-start.31 = (f32[64,1,2,128]{3,0,2,1:T(8,128)S(1)}, f32[64,1,2,128]{3,0,2,1:T(8,128)S(1)}, u32[]{:S(2)}, u32[]{:S(2)}) collective-permute-start(f32[64,1,2,128]{3,0,2,1:T(8,128)S(1)} %get-tuple-element.17), channel_id=1, source_target_pairs={{4,0},{8,4},{12,8},{16,12},{20,16},{24,20},{28,24},{32,28},{36,32}... | collective-permute-start | bytes 196616 | tf_op jit(solution)/shard_map/ppermute | solution.py:26
  207.4 3.9 %collective-permute-start.32 = (f32[64,6,1,128]{3,0,2,1:T(8,128)S(1)}, f32[64,6,1,128]{3,0,2,1:T(8,128)S(1)}, u32[]{:S(2)}, u32[]{:S(2)}) collective-permute-start(f32[64,6,1,128]{3,0,2,1:T(8,128)S(1)} %get-tuple-element.8), channel_id=1, source_target_pairs={{0,1},{1,2},{2,3},{4,5},{5,6},{6,7},{8,9},{9,10},{10,11},{12,13},{... | collective-permute-start | bytes 589832 | tf_op jit(solution)/shard_map/ppermute | solution.py:23
  208.7 6.4 %collective-permute-start.33 = (f32[64,6,1,128]{3,0,2,1:T(8,128)S(1)}, f32[64,6,1,128]{3,0,2,1:T(8,128)S(1)}, u32[]{:S(2)}, u32[]{:S(2)}) collective-permute-start(f32[64,6,1,128]{3,0,2,1:T(8,128)S(1)} %get-tuple-element.9), channel_id=1, source_target_pairs={{1,0},{2,1},{3,2},{5,4},{6,5},{7,6},{9,8},{10,9},{11,10},{13,12},{... | collective-permute-start | bytes 589832 | tf_op jit(solution)/shard_map/ppermute | solution.py:26
  217.2 6.4 %collective-permute-start.34 = (f32[64,1,2,128]{3,0,2,1:T(8,128)S(1)}, f32[64,1,2,128]{3,0,2,1:T(8,128)S(1)}, u32[]{:S(2)}, u32[]{:S(2)}) collective-permute-start(f32[64,1,2,128]{3,0,2,1:T(8,128)S(1)} %get-tuple-element.14), channel_id=1, source_target_pairs={{0,4},{4,8},{8,12},{12,16},{16,20},{20,24},{24,28},{28,32},{32,36}... | collective-permute-start | bytes 196616 | tf_op jit(solution)/shard_map/ppermute | solution.py:23
  220.3 8.9 %collective-permute-start.35 = (f32[64,1,2,128]{3,0,2,1:T(8,128)S(1)}, f32[64,1,2,128]{3,0,2,1:T(8,128)S(1)}, u32[]{:S(2)}, u32[]{:S(2)}) collective-permute-start(f32[64,1,2,128]{3,0,2,1:T(8,128)S(1)} %get-tuple-element.15), channel_id=1, source_target_pairs={{4,0},{8,4},{12,8},{16,12},{20,16},{24,20},{28,24},{32,28},{36,32}... | collective-permute-start | bytes 196616 | tf_op jit(solution)/shard_map/ppermute | solution.py:26
  229.2 6.2 %collective-permute-start.36 = (f32[64,6,1,128]{3,0,2,1:T(8,128)S(1)}, f32[64,6,1,128]{3,0,2,1:T(8,128)S(1)}, u32[]{:S(2)}, u32[]{:S(2)}) collective-permute-start(f32[64,6,1,128]{3,0,2,1:T(8,128)S(1)} %get-tuple-element.6), channel_id=1, source_target_pairs={{0,1},{1,2},{2,3},{4,5},{5,6},{6,7},{8,9},{9,10},{10,11},{12,13},{... | collective-permute-start | bytes 589832 | tf_op jit(solution)/shard_map/ppermute | solution.py:23
  232.9 6.4 %collective-permute-start.37 = (f32[64,6,1,128]{3,0,2,1:T(8,128)S(1)}, f32[64,6,1,128]{3,0,2,1:T(8,128)S(1)}, u32[]{:S(2)}, u32[]{:S(2)}) collective-permute-start(f32[64,6,1,128]{3,0,2,1:T(8,128)S(1)} %get-tuple-element.7), channel_id=1, source_target_pairs={{1,0},{2,1},{3,2},{5,4},{6,5},{7,6},{9,8},{10,9},{11,10},{13,12},{... | collective-permute-start | bytes 589832 | tf_op jit(solution)/shard_map/ppermute | solution.py:26
where the time goes:
time: 243 us; the launch traced here: 242 us
  starting transfers between devices  112 us (46%)
  waiting for transfers between devices  73.6 us (30%)
  matrix products  31.2 us (13%)
  blocking collectives  17.1 us (7%)
  local copies, waits for them, and re-layouts  4.58 us (2%)
    ppermute x11, waiting for transfers between devices, extended(): lax.ppermute(lax.slice_in_dim(block, 0, width, axis=dim), axis, backward)  57 us
    ppermute x16, starting transfers between devices, shifted(): return lax.ppermute(block, axis, route)  54.3 us
    ppermute x11, starting transfers between devices, extended(): lax.ppermute(lax.slice_in_dim(block, block.shape[dim] - width, None, axis...  35.2 us
    dot_general x72, matrix products, multiply(): jnp.tensordot(matrix, values, axes=1, precision=lax.Precision.HIGHEST)  29.7 us
    ppermute x11, starting transfers between devices, extended(): lax.ppermute(lax.slice_in_dim(block, 0, width, axis=dim), axis, backward)  22.4 us
    ppermute x16, waiting for transfers between devices, shifted(): return lax.ppermute(block, axis, route)  12.9 us
    all_gather x1, blocking collectives, shards(): lax.all_gather(coarse_source, 'gy', axis=2, tiled=True)  9.37 us
    all_gather x1, blocking collectives, shards(): lax.all_gather(coarse_coef, 'gy', axis=1, tiled=True)  7.7 us
  transfers between devices with their start and end apart: 38, of which 19 were waited for; matrix products, arithmetic and copies ran while one was open for 4% of the time, Pallas kernels for 0%

commit v1 on v0

v1 whole, which is shorter than its diff:
```python
import functools

import jax
import jax.numpy as jnp
from jax import lax
from jax.experimental import pallas as pl
from jax.experimental.pallas import tpu as pltpu
from jax.sharding import PartitionSpec as P

MESH = pl.DeviceIdType.MESH
F32 = jnp.float32
BF16 = jnp.bfloat16
OMEGA = 0.8
N = 64
LANES = 128
XM, XP, YM, YP, CC, ZM, ZP, SM = (64 * i for i in range(8))
FACES = (XM, XP, YM, YP, ZM, ZP)


def split(v):
    hi = v.astype(BF16)
    lo = (v - hi.astype(F32)).astype(BF16)
    return jnp.concatenate([hi, lo, hi], axis=0)


def exact_dot(a, b):
    return jnp.dot(a, b, precision=lax.Precision.HIGHEST, preferred_element_type=F32)


def widen(w):
    hi = w.astype(BF16)
    lo = (w - hi.astype(F32)).astype(BF16)
    return jnp.concatenate([hi, hi, lo], axis=1)


def kernel(ngx, ngy, src, kap, diag, faces, smooth, prol, sol, res,
           q0, u1, u2, u3, q1, u11, u21, e1, q2, u12, u22, e2, pp, rr,
           wm, wl, wb, wr, wp,
           s_q0, r_q0, s_u2, r_u2, s_u2b, r_u2b, s_g, r_g, s_rl, r_rl, s_q2, r_q2, s_u21, r_u21):
    gx, gy = lax.axis_index("gx"), lax.axis_index("gy")

    def inside(dx, dy):
        ok = None
        for at, d, n in ((gx, dx, ngx), (gy, dy, ngy)):
            if d:
                c = (at + d >= 0) & (at + d < n)
                ok = c if ok is None else ok & c
        return ok

    barrier = pltpu.get_barrier_semaphore()
    partners = [(d, 0) for d in (-3, -2, -1, 1, 2, 3)] + [(0, d) for d in (-3, -2, -1, 1, 2, 3)]
    partners += [(a, b) for a in (-1, 1) for b in (-1, 1)]
    for dx, dy in partners:
        @pl.when(inside(dx, dy))
        def _():
            pl.semaphore_signal(barrier, inc=1, device_id=(gx + dx, gy + dy), device_id_type=MESH)
    for y in range(2):
        for x in range(4):
            c = x * 2 + y
            q0[1 + y, 1 + x] = src[pl.ds(c, N, stride=8), :] / kap[pl.ds(c, 1), :]
    peers = 0
    for dx, dy in partners:
        peers = peers + inside(dx, dy).astype(jnp.int32)
    pl.semaphore_wait(barrier, peers)

    def remote(s, d, ssem, rsem, dx, dy):
        return pltpu.make_async_remote_copy(
            src_ref=s, dst_ref=d, send_sem=ssem, recv_sem=rsem,
            device_id=(gx + dx, gy + dy), device_id_type=MESH)

    def send(s, d, ssem, rsem, dx, dy, cond=None):
        ok = inside(dx, dy) if cond is None else cond

        @pl.when(ok)
        def _():
            remote(s, d, ssem, rsem, dx, dy).start()

    def receive(d, ssem, rsem, dx, dy, cond=None):
        ok = inside(dx, dy) if cond is None else cond

        @pl.when(ok)
        def _():
            remote(d, d, ssem, rsem, dx, dy).wait_recv()

    def clear(ref, dx, dy):
        @pl.when(jnp.logical_not(inside(dx, dy)))
        def _():
            ref[...] = jnp.zeros(ref.shape, F32)

    def first_faces(buf, oy, ox):
        return [
            (buf.at[oy + 1, pl.ds(ox, 4)], buf.at[oy - 1, pl.ds(ox, 4)], 0, 1),
            (buf.at[oy, pl.ds(ox, 4)], buf.at[oy + 2, pl.ds(ox, 4)], 0, -1),
            (buf.at[pl.ds(oy, 2), ox + 3], buf.at[pl.ds(oy, 2), ox - 1], 1, 0),
            (buf.at[pl.ds(oy, 2), ox], buf.at[pl.ds(oy, 2), ox + 4], -1, 0),
        ]

    def second_faces(buf, oy, ox):
        return [
            (buf.at[oy, pl.ds(ox, 4)], buf.at[oy - 2, pl.ds(ox, 4)], 0, 1),
            (buf.at[oy + 1, pl.ds(ox, 4)], buf.at[oy + 3, pl.ds(ox, 4)], 0, -1),
            (buf.at[pl.ds(oy, 2), ox + 2], buf.at[pl.ds(oy, 2), ox - 2], 1, 0),
            (buf.at[pl.ds(oy, 2), ox + 1], buf.at[pl.ds(oy, 2), ox + 5], -1, 0),
            (buf.at[oy + 1, ox + 3], buf.at[oy - 1, ox - 1], 1, 1),
            (buf.at[oy + 1, ox], buf.at[oy - 1, ox + 4], -1, 1),
            (buf.at[oy, ox + 3], buf.at[oy + 2, ox - 1], 1, -1),
            (buf.at[oy, ox], buf.at[oy + 2, ox + 4], -1, -1),
        ]

    def send_all(faces_of, ssem, rsem):
        for i, (s, d, dx, dy) in enumerate(faces_of):
            send(s, d, ssem.at[i], rsem.at[i], dx, dy)

    def receive_all(faces_of, ssem, rsem):
        for i, (s, d, dx, dy) in enumerate(faces_of):
            receive(d, ssem.at[i], rsem.at[i], -dx, -dy)

    q0_faces = first_faces(q0, 1, 1)
    u2_faces = first_faces(u2, 2, 2)
    u2_more = second_faces(u2, 2, 2)
    send_all(q0_faces, s_q0, r_q0)

    s8 = OMEGA * smooth[...]
    eye = (lax.broadcasted_iota(jnp.int32, (N, N), 0) == lax.broadcasted_iota(jnp.int32, (N, N), 1)).astype(F32)
    wm[pl.ds(SM, N), :] = widen(s8)
    for i, at in enumerate(FACES):
        f = faces[i]
        wb[pl.ds(at, N), :] = widen(-f)
        sf = exact_dot(s8, f)
        wl[pl.ds(at, N), :] = widen(sf)
        wm[pl.ds(at, N), :] = widen(exact_dot(sf, s8))
    d = diag[...]
    wb[pl.ds(CC, N), :] = widen(d)
    lc = eye - exact_dot(s8, d)
    wl[pl.ds(CC, N), :] = widen(lc)
    wm[pl.ds(CC, N), :] = widen(s8 + exact_dot(lc, s8))
    for i in range(4):
        p = prol[i]
        wp[pl.ds(N * i, N), :] = widen(p)
        wr[pl.ds(N * i, N), :] = widen(0.25 * p.T)

    for buf, group in ((q0, q0_faces), (u2, u2_faces), (u2, u2_more)):
        for s, dst, dx, dy in group:
            clear(dst, -dx, -dy)
    clear(q1.at[pl.ds(0, 2)], -1, 0)
    clear(q1.at[pl.ds(4, 2)], 1, 0)
    clear(u21.at[0], -1, 0)
    clear(u21.at[5], 1, 0)
    for dd in (1, 2, 3):
        clear(q2.at[3 - dd], -dd, 0)
        clear(q2.at[3 + dd], dd, 0)
    e1[:, 0] = jnp.zeros((4, N, LANES), F32)
    e1[:, 5] = jnp.zeros((4, N, LANES), F32)

    lane = lax.broadcasted_iota(jnp.int32, (N, LANES), 1)
    not_first, not_last = lane > 0, lane < LANES - 1

    def apply(w, row, rows, load, cols, at):
        pair = jnp.concatenate([split(load(cols[0])), split(load(cols[1]))], axis=1)
        out = jnp.dot(w[pl.ds(row, rows), :], pair, preferred_element_type=F32)
        pp[at[0], pl.ds(row, rows), :] = out[:, :LANES]
        pp[at[1], pl.ds(row, rows), :] = out[:, LANES:]

    def gathered(c, sx, sy, ym=True, yp=True):
        t = pp[c, pl.ds(CC, N), :]
        t = t + pp[c - sx, pl.ds(XM, N), :] + pp[c + sx, pl.ds(XP, N), :]
        if ym:
            t = t + pp[c - sy, pl.ds(YM, N), :]
        if yp:
            t = t + pp[c + sy, pl.ds(YP, N), :]
        t = t + jnp.where(not_first, pltpu.roll(pp[c, pl.ds(ZM, N), :], 1, 1), 0.0)
        t = t + jnp.where(not_last, pltpu.roll(pp[c, pl.ds(ZP, N), :], LANES - 1, 1), 0.0)
        return t

    def loop(n, body):
        def step(i, carry):
            body(i)
            return carry
        lax.fori_loop(0, n, step, 0)

    def fine_at(y, x):
        return (y + 2) * 8 + x + 2

    def fine_own(w, rows, buf, oy, ox):
        def body(i):
            y, x = i // 2, (i % 2) * 2
            apply(w, 0, rows, lambda c: buf[oy + c[0], ox + c[1]], ((y, x), (y, x + 1)),
                  (fine_at(y, x), fine_at(y, x + 1)))
        loop(4, body)

    def fine_edges(w, buf, oy, ox):
        def load(c):
            return buf[oy + c[0], ox + c[1]]

        def body_x(y):
            apply(w, XM, 128, load, ((y, -1), (y, 4)), (fine_at(y, -1), fine_at(y, 4)))
        loop(2, body_x)

        def body_y(x):
            apply(w, YM, 128, load, ((-1, x), (2, x)), (fine_at(-1, x), fine_at(2, x)))
        loop(4, body_y)

    fine_own(wm, 512, q0, 1, 1)
    receive_all(q0_faces, s_q0, r_q0)
    fine_edges(wm, q0, 1, 1)

    def sum_u2(i):
        y, x = i // 4, i % 4
        c = fine_at(y, x)
        u2[2 + y, 2 + x] = gathered(c, 1, 8)
        u1[1 + y, 1 + x] = pp[c, pl.ds(SM, N), :]
    loop(8, sum_u2)
    send_all(u2_faces, s_u2, r_u2)

    fine_own(wb, 448, u2, 2, 2)

    def ring_u1(y, x, y2, x2):
        pair = jnp.concatenate([split(q0[1 + y, 1 + x]), split(q0[1 + y2, 1 + x2])], axis=1)
        out = jnp.dot(wm[pl.ds(SM, N), :], pair, preferred_element_type=F32)
        u1[1 + y, 1 + x] = out[:, :LANES]
        u1[1 + y2, 1 + x2] = out[:, LANES:]
    loop(2, lambda y: ring_u1(y, -1, y, 4))
    loop(4, lambda x: ring_u1(-1, x, 2, x))
    receive_all(u2_faces, s_u2, r_u2)
    fine_edges(wb, u2, 2, 2)

    def sum_r0(i):
        y, x = i // 4, i % 4
        t = gathered(fine_at(y, x), 1, 8)
        k = kap[pl.ds(x * 2 + y, 1), :]
        rr[i] = split((q0[1 + y, 1 + x] - t) * k)
    loop(8, sum_r0)

    def restrict(index):
        total = None
        for child in range(4):
            pair = jnp.concatenate([rr[index(0, child)], rr[index(1, child)]], axis=1)
            part = jnp.dot(wr[pl.ds(N * child, N), :], pair, preferred_element_type=F32)
            total = part if total is None else total + part
        return total[:, :LANES], total[:, LANES:]

    coarse = restrict(lambda at, child: (child % 2) * 4 + 2 * at + child // 2)
    for at in range(2):
        k1 = kap[pl.ds(4 * at, 1), :] + kap[pl.ds(4 * at + 1, 1), :]
        k1 = (k1 + (kap[pl.ds(4 * at + 2, 1), :] + kap[pl.ds(4 * at + 3, 1), :])) * 0.25
        q1[2 + at, gy, pl.ds(0, N), :] = coarse[at] / k1
        q1[2 + at, gy, pl.ds(N, 8), :] = jnp.broadcast_to(k1, (8, LANES))

    for j in range(ngy):
        own = q1.at[pl.ds(2, 2), gy]
        cond = gy != j

        @pl.when(cond)
        def _():
            pltpu.make_async_remote_copy(
                src_ref=own, dst_ref=own, send_sem=s_g.at[j], recv_sem=r_g.at[gy],
                device_id=(gx, j), device_id_type=MESH).start()

    def relay(j):
        block = q1.at[pl.ds(2, 2), j]
        for i, (dx, at) in enumerate(((1, 0), (-1, 4))):
            @pl.when(inside(dx, 0))
            def _():
                remote(block, q1.at[pl.ds(at, 2), j], s_rl.at[i, j], r_rl.at[i, j], dx, 0).start()

    relay(gy)
    send_all(u2_more, s_u2b, r_u2b)

    def arrive(j):
        block = q1.at[pl.ds(2, 2), j]
        pltpu.make_async_remote_copy(
            src_ref=block, dst_ref=block, send_sem=s_g.at[j], recv_sem=r_g.at[j],
            device_id=(gx, j), device_id_type=MESH).wait_recv()
        relay(j)
    for dd in (1, -1, 2, -2, 3, -3):
        @pl.when(inside(0, dd))
        def _():
            arrive(gy + dd)

    def coarse_own(w, rows, load, first, planes):
        def body(i):
            c = 4 * first + 2 * i
            apply(w, 0, rows, load, (c, c + 1), (c, c + 1))
        loop(2 * planes, body)

    def coarse_edges(w, load, low, high):
        def body(y):
            c, e = 4 * low + y, 4 * high + y
            apply(w, XM, 128, load, (c, e), (c, e))
        loop(4, body)

    def load_q1(c):
        return q1[c // 4, c % 4, pl.ds(0, N), :]

    def load_u21(c):
        return u21[c // 4, c % 4]

    coarse_own(wm, 512, load_q1, 2, 2)
    for j in range(ngy):
        for i, (dx, at) in enumerate(((1, 0), (-1, 4))):
            @pl.when(inside(-dx, 0))
            def _():
                block = q1.at[pl.ds(at, 2), j]
                remote(block, block, s_rl.at[i, j], r_rl.at[i, j], -dx, 0).wait_recv()
    coarse_own(wm, 512, load_q1, 1, 1)
    coarse_own(wm, 512, load_q1, 4, 1)
    coarse_edges(wm, load_q1, 0, 5)

    def keep(ok):
        return jnp.where(ok, 1.0, 0.0).astype(F32)

    def present(offset):
        return keep((gx + offset >= 0) & (gx + offset < ngx))

    def device_of(x):
        return (x // 2) - 1

    def sum_u21(x):
        m = present(device_of(x))
        for y in range(4):
            c = 4 * x + y
            u21[x, y] = m * gathered(c, 4, 1, y > 0, y < 3)
            u11[x, y] = m * pp[c, pl.ds(SM, N), :]
    loop(4, lambda i: sum_u21(i + 1))

    coarse_own(wb, 448, load_u21, 2, 2)
    coarse_edges(wb, load_u21, 1, 4)

    def sum_r1(x):
        for y in range(4):
            t = gathered(4 * x + y, 4, 1, y > 0, y < 3)
            k1 = q1[x, y, pl.ds(N, 1), :]
            rr[(x - 2) * 4 + y] = split((q1[x, y, pl.ds(0, N), :] - t) * k1)
    loop(2, lambda i: sum_r1(i + 2))
    coarse2 = restrict(lambda at, child: (child // 2) * 4 + 2 * at + child % 2)
    for at in range(2):
        k2 = q1[2, 2 * at, pl.ds(N, 1), :] + q1[2, 2 * at + 1, pl.ds(N, 1), :]
        k2 = (k2 + (q1[3, 2 * at, pl.ds(N, 1), :] + q1[3, 2 * at + 1, pl.ds(N, 1), :])) * 0.25
        q2[3, at] = coarse2[at] / k2

    q2_moves = [(q2.at[3], q2.at[3 - dd], dd, 0) for dd in (1, -1, 2, -2, 3, -3)]
    send_all(q2_moves, s_q2, r_q2)
    u21_moves = [(u21.at[2], u21.at[0], 1, 0), (u21.at[3], u21.at[5], -1, 0)]
    send_all(u21_moves, s_u21, r_u21)

    def load_q2(c):
        return q2[c // 2, c % 2]

    def load_u22(c):
        return u22[c // 2, c % 2]

    def last_own(w, rows, load, first, planes):
        def body(i):
            c = 2 * first + 2 * i
            apply(w, 0, rows, load, (c, c + 1), (c, c + 1))
        loop(planes, body)

    def last_edges(w, load, low, high):
        def body(y):
            c, e = 2 * low + y, 2 * high + y
            apply(w, XM, 128, load, (c, e), (c, e))
        loop(2, body)

    last_own(wm, 512, load_q2, 3, 1)
    receive_all(q2_moves, s_q2, r_q2)
    last_own(wm, 512, load_q2, 1, 2)
    last_own(wm, 512, load_q2, 4, 2)
    last_edges(wm, load_q2, 0, 6)

    def sum_u22(x):
        m = present(x - 3)
        for y in range(2):
            u22[x, y] = m * gathered(2 * x + y, 2, 1, y > 0, y < 1)
            u12[x, y] = pp[2 * x + y, pl.ds(SM, N), :]
    loop(5, lambda i: sum_u22(i + 1))
    last_own(wl, 448, load_u22, 2, 3)
    last_edges(wl, load_u22, 1, 5)

    def sum_e2(x):
        m = present(x - 3)
        for y in range(2):
            e2[x - 2, y] = m * (u12[x, y] + gathered(2 * x + y, 2, 1, y > 0, y < 1))
    loop(3, lambda i: sum_e2(i + 2))

    receive_all(u21_moves, s_u21, r_u21)

    def prolong(load):
        pair = jnp.concatenate([split(load(0)), split(load(1))], axis=1)
        out = jnp.dot(wp[...], pair, preferred_element_type=F32)
        return lambda at, child: out[N * child:N * (child + 1), LANES * at:LANES * (at + 1)]

    for i, (s, dst, dx, dy) in enumerate(u21_moves):
        @pl.when(inside(dx, dy))
        def _():
            remote(s, dst, s_u21.at[i], r_u21.at[i], dx, dy).wait_send()

    def lift1(x2):
        part = prolong(lambda y: e2[x2, y])
        for y2 in range(2):
            for child in range(4):
                x, y = 2 * x2 + child // 2, 2 * y2 + child % 2
                u21[x, y] = u21[x, y] + part(y2, child)
    loop(3, lift1)
    coarse_own(wl, 448, load_u21, 1, 4)
    coarse_edges(wl, load_u21, 0, 5)

    def sum_e1(x):
        m = present(device_of(x))
        for y in range(4):
            e1[x - 1, 1 + y] = m * (u11[x, y] + gathered(4 * x + y, 4, 1, y > 0, y < 3))
    loop(4, lambda i: sum_e1(i + 1))

    for i, (s, dst, dx, dy) in enumerate(u2_faces):
        @pl.when(inside(dx, dy))
        def _():
            remote(s, dst, s_u2.at[i], r_u2.at[i], dx, dy).wait_send()
    receive_all(u2_more, s_u2b, r_u2b)
    for i, (s, dst, dx, dy) in enumerate(u2_more):
        @pl.when(inside(dx, dy))
        def _():
            remote(s, dst, s_u2b.at[i], r_u2b.at[i], dx, dy).wait_send()

    wanted = {(y, x) for y in range(-2, 4) for x in range(-2, 6)
              if max(0, -y, y - 1) + max(0, -x, x - 3) <= 2}
    for j in range(3):
        for xp in range(2):
            part = prolong(lambda i: e1[2 * xp + i, gy + j])
            for i in range(2):
                for child in range(4):
                    x = 2 * (2 * xp + i - 1) + child // 2
                    y = 2 * (j - 1) + child % 2
                    if (y, x) in wanted:
                        u2[2 + y, 2 + x] = u2[2 + y, 2 + x] + part(i, child)

    def load_u2(c):
        return u2[2 + c[0], 2 + c[1]]

    def both(w, row, rows, c, e):
        apply(w, row, rows, load_u2, (c, e), (fine_at(*c), fine_at(*e)))

    def rows_wide(i):
        y, x = i // 3, (i % 3) * 2 - 1
        both(wl, 0, 448, (y, x), (y, x + 1))
    loop(6, rows_wide)

    def rows_short(i):
        y, x = (i // 2) * 3 - 1, (i % 2) * 2
        both(wl, 0, 448, (y, x), (y, x + 1))
    loop(4, rows_short)
    loop(2, lambda y: both(wl, XM, 128, (y, -2), (y, 5)))
    loop(4, lambda x: both(wl, YM, 128, (-2, x), (3, x)))
    loop(2, lambda i: both(wl, 0, 256, (3 * i - 1, -1), (3 * i - 1, 4)))

    def sum_u3(y, x, m=None):
        v = u1[1 + y, 1 + x] + gathered(fine_at(y, x), 1, 8)
        u3[1 + y, 1 + x] = v if m is None else m * v
        return v

    def own_u3(i):
        y, x = i // 4, i % 4
        v = sum_u3(y, x)
        sol[pl.ds(x * 2 + y, N, stride=8), :] = v
    loop(8, own_u3)
    loop(2, lambda y: sum_u3(y, -1, present(-1)))
    loop(2, lambda y: sum_u3(y, 4, present(1)))
    loop(4, lambda x: sum_u3(-1, x, keep(gy > 0)))
    loop(4, lambda x: sum_u3(2, x, keep(gy < ngy - 1)))
    fine_own(wb, 448, u3, 1, 1)
    fine_edges(wb, u3, 1, 1)

    def final(i):
        y, x = i // 4, i % 4
        c = x * 2 + y
        t = gathered(fine_at(y, x), 1, 8)
        res[pl.ds(c, N, stride=8), :] = src[pl.ds(c, N, stride=8), :] - kap[pl.ds(c, 1), :] * t
    loop(8, final)

    for group, ssem, rsem in ((q0_faces, s_q0, r_q0), (q2_moves, s_q2, r_q2)):
        for i, (s, dst, dx, dy) in enumerate(group):
            @pl.when(inside(dx, dy))
            def _():
                remote(s, dst, ssem.at[i], rsem.at[i], dx, dy).wait_send()
    for j in range(ngy):
        block = q1.at[pl.ds(2, 2), j]

        @pl.when(gy != j)
        def _():
            pltpu.make_async_remote_copy(
                src_ref=block, dst_ref=block, send_sem=s_g.at[j], recv_sem=r_g.at[j],
                device_id=(gx, j), device_id_type=MESH).wait_send()
        for i, (dx, at) in enumerate(((1, 0), (-1, 4))):
            @pl.when(inside(dx, 0))
            def _():
                remote(block, q1.at[pl.ds(at, 2), j], s_rl.at[i, j], r_rl.at[i, j], dx, 0).wait_send()


def solution(mesh):
    ngx, ngy = mesh.shape["gx"], mesh.shape["gy"]

    def shards(source, conductivity, diag_block, face_blocks, smoother, prolong):
        dma = pltpu.SemaphoreType.DMA
        col = (N, LANES)
        scratch = [
            pltpu.VMEM((4, 6) + col, F32),
            pltpu.VMEM((4, 6) + col, F32),
            pltpu.VMEM((6, 8) + col, F32),
            pltpu.VMEM((4, 6) + col, F32),
            pltpu.VMEM((6, 4, N + 8, LANES), F32),
            pltpu.VMEM((6, 4) + col, F32),
            pltpu.VMEM((6, 4) + col, F32),
            pltpu.VMEM((4, 6) + col, F32),
            pltpu.VMEM((7, 2) + col, F32),
            pltpu.VMEM((7, 2) + col, F32),
            pltpu.VMEM((7, 2) + col, F32),
            pltpu.VMEM((3, 2) + col, F32),
            pltpu.VMEM((48, 512, LANES), F32),
            pltpu.VMEM((8, 192, LANES), BF16),
            pltpu.VMEM((512, 192), BF16),
            pltpu.VMEM((448, 192), BF16),
            pltpu.VMEM((448, 192), BF16),
            pltpu.VMEM((256, 192), BF16),
            pltpu.VMEM((256, 192), BF16),
            dma((4,)), dma((4,)), dma((4,)), dma((4,)), dma((8,)), dma((8,)),
            dma((4,)), dma((4,)), dma((2, 4)), dma((2, 4)), dma((6,)), dma((6,)), dma((2,)), dma((2,)),
        ]
        shape = source.shape
        flat = jax.ShapeDtypeStruct((N * 8, LANES), F32)
        vmem = pl.BlockSpec(memory_space=pltpu.VMEM)
        sol, res = pl.pallas_call(
            functools.partial(kernel, ngx, ngy),
            out_shape=(flat, flat),
            in_specs=[vmem] * 6,
            out_specs=(vmem, vmem),
            scratch_shapes=scratch,
            compiler_params=pltpu.CompilerParams(
                collective_id=0, has_side_effects=True, vmem_limit_bytes=40 << 20),
            cost_estimate=pl.CostEstimate(flops=10**9, bytes_accessed=10**6, transcendentals=0),
        )(source.reshape(N * 8, LANES), conductivity.reshape(8, LANES),
          diag_block, face_blocks, smoother, prolong)
        return sol.reshape(shape), res.reshape(shape)

    return jax.shard_map(
        shards,
        mesh=mesh,
        in_specs=(P(None, "gx", "gy", None), P("gx", "gy", None), P(), P(), P(), P()),
        out_specs=(P(None, "gx", "gy", None), P(None, "gx", "gy", None)),
        check_vma=False,
    )
```

time: 243 us -> 63 us (0.26)
  the two profiles are of different devices: /device:TPU:249 before, /device:TPU:247 now
where the time goes in v1:
time: 63 us; the launch traced here: 62.7 us
  Pallas kernels  55.6 us (88%)
  local copies, waits for them, and re-layouts  6.38 us (10%)
  between operations  0.65 us (1%)
    pallas_call x1, Pallas kernels, shards(): pl.pallas_call(functools.partial(kernel, ngx, ngy), out_shape=(flat, flat...  55.6 us
    unnamed x14, local copies, waits for them, and re-layouts  6.38 us

profile of v1, /device:TPU:247, one launch (start us, length us, event | category | flops | bytes accessed | tf_op | source)
XLA Modules:
  0.0 62.7 jit_solution(2091876875065302233)
XLA Ops:
  0.6 0.0 copy-start
  0.6 0.9 %copy-done = f32[64,4,2,128]{3,2,1,0:T(2,128)S(1)} copy-done((f32[64,4,2,128]{3,2,1,0:T(2,128)S(1)}, f32[64,4,2,128]{3,2,1,0:T(2,128)}, u32[]{:S(2)}) %copy-start) | copy-done | bytes 262168
  1.6 0.0 copy-start.1
  1.6 0.9 %copy-done.1 = f32[6,64,64]{2,1,0:T(8,128)S(1)} copy-done((f32[6,64,64]{2,1,0:T(8,128)S(1)}, f32[6,64,64]{2,1,0:T(8,128)}, u32[]{:S(2)}) %copy-start.1) | copy-done | bytes 98328
  2.5 0.0 copy-start.2
  2.5 0.9 %copy-done.2 = f32[4,64,64]{2,1,0:T(8,128)S(1)} copy-done((f32[4,64,64]{2,1,0:T(8,128)S(1)}, f32[4,64,64]{2,1,0:T(8,128)}, u32[]{:S(2)}) %copy-start.2) | copy-done | bytes 65560
  3.4 0.0 copy-start.3
  3.4 0.8 %copy-done.3 = f32[64,64]{1,0:T(8,128)S(1)} copy-done((f32[64,64]{1,0:T(8,128)S(1)}, f32[64,64]{1,0:T(8,128)}, u32[]{:S(2)}) %copy-start.3) | copy-done | bytes 16408
  4.2 0.0 copy-start.4
  4.2 0.8 %copy-done.4 = f32[64,64]{1,0:T(8,128)S(1)} copy-done((f32[64,64]{1,0:T(8,128)S(1)}, f32[64,64]{1,0:T(8,128)}, u32[]{:S(2)}) %copy-start.4) | copy-done | bytes 16408
  4.9 0.0 copy-start.5
  4.9 0.7 %copy-done.5 = f32[4,2,128]{2,1,0:T(2,128)S(1)} copy-done((f32[4,2,128]{2,1,0:T(2,128)S(1)}, f32[4,2,128]{2,1,0:T(2,128)}, u32[]{:S(2)}) %copy-start.5) | copy-done | bytes 4120
  5.6 55.6 %shard_map.77 = (f32[512,128]{1,0:T(8,128)S(1)}, f32[512,128]{1,0:T(8,128)S(1)}) custom-call(f32[512,128]{1,0:T(8,128)S(1)} %bitcast.6, f32[8,128]{1,0:T(8,128)S(1)} %bitcast.7, f32[64,64]{1,0:T(8,128)S(1)} %copy-done.3, f32[6,64,64]{2,1,0:T(8,128)S(1)} %copy-done.1, f32[64,64]{1,0:T(8,128)S(1)} %copy-done.4, f32[4,64,64]{2,1,0:T(8,128)S(1)} %copy-done.2), custom_call_target="tpu_custom_call" | custom-call | flops 1000000000 | bytes 1000000 | tf_op jit(solution)/shard_map/pallas_call | solution.py:529
  61.3 0.7 %copy.10 = f32[64,4,2,128]{3,2,1,0:T(2,128)} copy(f32[64,4,2,128]{3,2,1,0:T(2,128)S(1)} %bitcast.5) | data formatting | bytes 524288
  62.0 0.7 %copy.11 = f32[64,4,2,128]{3,2,1,0:T(2,128)} copy(f32[64,4,2,128]{3,2,1,0:T(2,128)S(1)} %bitcast.4) | data formatting | bytes 524288
Async XLA Ops:
  0.6 1.0 %copy-start = (f32[64,4,2,128]{3,2,1,0:T(2,128)S(1)}, f32[64,4,2,128]{3,2,1,0:T(2,128)}, u32[]{:S(2)}) copy-start(f32[64,4,2,128]{3,2,1,0:T(2,128)} %param.6) | copy-start | bytes 786436
  1.6 0.9 %copy-start.1 = (f32[6,64,64]{2,1,0:T(8,128)S(1)}, f32[6,64,64]{2,1,0:T(8,128)}, u32[]{:S(2)}) copy-start(f32[6,64,64]{2,1,0:T(8,128)} %faces.1) | copy-start | bytes 294916
  2.5 0.9 %copy-start.2 = (f32[4,64,64]{2,1,0:T(8,128)S(1)}, f32[4,64,64]{2,1,0:T(8,128)}, u32[]{:S(2)}) copy-start(f32[4,64,64]{2,1,0:T(8,128)} %prol.1) | copy-start | bytes 196612
  3.4 0.8 %copy-start.3 = (f32[64,64]{1,0:T(8,128)S(1)}, f32[64,64]{1,0:T(8,128)}, u32[]{:S(2)}) copy-start(f32[64,64]{1,0:T(8,128)} %diag.1) | copy-start | bytes 49156
  4.2 0.8 %copy-start.4 = (f32[64,64]{1,0:T(8,128)S(1)}, f32[64,64]{1,0:T(8,128)}, u32[]{:S(2)}) copy-start(f32[64,64]{1,0:T(8,128)} %smooth.1) | copy-start | bytes 49156
  4.9 0.7 %copy-start.5 = (f32[4,2,128]{2,1,0:T(2,128)S(1)}, f32[4,2,128]{2,1,0:T(2,128)}, u32[]{:S(2)}) copy-start(f32[4,2,128]{2,1,0:T(2,128)} %param.7) | copy-start | bytes 12292

commit v2 on v1

--- a/solution.py
+++ b/solution.py
@@ -173,10 +173,8 @@
         return t
 
     def loop(n, body):
-        def step(i, carry):
+        for i in range(n):
             body(i)
-            return carry
-        lax.fori_loop(0, n, step, 0)
 
     def fine_at(y, x):
         return (y + 2) * 8 + x + 2

time: 63 us -> 46.1 us (0.73)
  the two profiles are of different devices: /device:TPU:247 before, /device:TPU:262 now
where the time goes in v2:
time: 46.1 us; the launch traced here: 45.7 us
  Pallas kernels  38.7 us (84%)
  local copies, waits for them, and re-layouts  6.38 us (14%)
  between operations  0.65 us (1%)
    pallas_call x1, Pallas kernels, shards(): pl.pallas_call(functools.partial(kernel, ngx, ngy), out_shape=(flat, flat...  38.7 us
    unnamed x14, local copies, waits for them, and re-layouts  6.38 us

profile of v2, /device:TPU:262, one launch (start us, length us, event | category | flops | bytes accessed | tf_op | source)
XLA Modules:
  0.0 45.7 jit_solution(13933164829365379256)
XLA Ops:
  0.6 0.0 copy-start
  0.6 0.9 %copy-done = f32[64,4,2,128]{3,2,1,0:T(2,128)S(1)} copy-done((f32[64,4,2,128]{3,2,1,0:T(2,128)S(1)}, f32[64,4,2,128]{3,2,1,0:T(2,128)}, u32[]{:S(2)}) %copy-start) | copy-done | bytes 262168
  1.6 0.0 copy-start.1
  1.6 0.9 %copy-done.1 = f32[6,64,64]{2,1,0:T(8,128)S(1)} copy-done((f32[6,64,64]{2,1,0:T(8,128)S(1)}, f32[6,64,64]{2,1,0:T(8,128)}, u32[]{:S(2)}) %copy-start.1) | copy-done | bytes 98328
  2.5 0.0 copy-start.2
  2.5 0.9 %copy-done.2 = f32[4,64,64]{2,1,0:T(8,128)S(1)} copy-done((f32[4,64,64]{2,1,0:T(8,128)S(1)}, f32[4,64,64]{2,1,0:T(8,128)}, u32[]{:S(2)}) %copy-start.2) | copy-done | bytes 65560
  3.4 0.0 copy-start.3
  3.4 0.8 %copy-done.3 = f32[64,64]{1,0:T(8,128)S(1)} copy-done((f32[64,64]{1,0:T(8,128)S(1)}, f32[64,64]{1,0:T(8,128)}, u32[]{:S(2)}) %copy-start.3) | copy-done | bytes 16408
  4.2 0.0 copy-start.4
  4.2 0.8 %copy-done.4 = f32[64,64]{1,0:T(8,128)S(1)} copy-done((f32[64,64]{1,0:T(8,128)S(1)}, f32[64,64]{1,0:T(8,128)}, u32[]{:S(2)}) %copy-start.4) | copy-done | bytes 16408
  4.9 0.0 copy-start.5
  4.9 0.7 %copy-done.5 = f32[4,2,128]{2,1,0:T(2,128)S(1)} copy-done((f32[4,2,128]{2,1,0:T(2,128)S(1)}, f32[4,2,128]{2,1,0:T(2,128)}, u32[]{:S(2)}) %copy-start.5) | copy-done | bytes 4120
  5.6 38.7 %shard_map.77 = (f32[512,128]{1,0:T(8,128)S(1)}, f32[512,128]{1,0:T(8,128)S(1)}) custom-call(f32[512,128]{1,0:T(8,128)S(1)} %bitcast.6, f32[8,128]{1,0:T(8,128)S(1)} %bitcast.7, f32[64,64]{1,0:T(8,128)S(1)} %copy-done.3, f32[6,64,64]{2,1,0:T(8,128)S(1)} %copy-done.1, f32[64,64]{1,0:T(8,128)S(1)} %copy-done.4, f32[4,64,64]{2,1,0:T(8,128)S(1)} %copy-done.2), custom_call_target="tpu_custom_call" | custom-call | flops 1000000000 | bytes 1000000 | tf_op jit(solution)/shard_map/pallas_call | solution.py:527
  44.3 0.7 %copy.10 = f32[64,4,2,128]{3,2,1,0:T(2,128)} copy(f32[64,4,2,128]{3,2,1,0:T(2,128)S(1)} %bitcast.5) | data formatting | bytes 524288
  45.0 0.7 %copy.11 = f32[64,4,2,128]{3,2,1,0:T(2,128)} copy(f32[64,4,2,128]{3,2,1,0:T(2,128)S(1)} %bitcast.4) | data formatting | bytes 524288
Async XLA Ops:
  0.6 1.0 %copy-start = (f32[64,4,2,128]{3,2,1,0:T(2,128)S(1)}, f32[64,4,2,128]{3,2,1,0:T(2,128)}, u32[]{:S(2)}) copy-start(f32[64,4,2,128]{3,2,1,0:T(2,128)} %param.6) | copy-start | bytes 786436
  1.6 0.9 %copy-start.1 = (f32[6,64,64]{2,1,0:T(8,128)S(1)}, f32[6,64,64]{2,1,0:T(8,128)}, u32[]{:S(2)}) copy-start(f32[6,64,64]{2,1,0:T(8,128)} %faces.1) | copy-start | bytes 294916
  2.5 0.9 %copy-start.2 = (f32[4,64,64]{2,1,0:T(8,128)S(1)}, f32[4,64,64]{2,1,0:T(8,128)}, u32[]{:S(2)}) copy-start(f32[4,64,64]{2,1,0:T(8,128)} %prol.1) | copy-start | bytes 196612
  3.4 0.8 %copy-start.3 = (f32[64,64]{1,0:T(8,128)S(1)}, f32[64,64]{1,0:T(8,128)}, u32[]{:S(2)}) copy-start(f32[64,64]{1,0:T(8,128)} %diag.1) | copy-start | bytes 49156
  4.2 0.8 %copy-start.4 = (f32[64,64]{1,0:T(8,128)S(1)}, f32[64,64]{1,0:T(8,128)}, u32[]{:S(2)}) copy-start(f32[64,64]{1,0:T(8,128)} %smooth.1) | copy-start | bytes 49156
  4.9 0.7 %copy-start.5 = (f32[4,2,128]{2,1,0:T(2,128)S(1)}, f32[4,2,128]{2,1,0:T(2,128)}, u32[]{:S(2)}) copy-start(f32[4,2,128]{2,1,0:T(2,128)} %param.7) | copy-start | bytes 12292

commit v3 on v2

v3 whole, which is shorter than its diff:
```python
import functools

import jax
import jax.numpy as jnp
from jax import lax
from jax.experimental import pallas as pl
from jax.experimental.pallas import tpu as pltpu
from jax.sharding import PartitionSpec as P

MESH = pl.DeviceIdType.MESH
F32 = jnp.float32
BF16 = jnp.bfloat16
OMEGA = 0.8
N = 64
LANES = 128
XM, XP, YM, YP, CC, ZM, ZP, SM = (64 * i for i in range(8))
FACES = (XM, XP, YM, YP, ZM, ZP)


def split(v):
    hi = v.astype(BF16)
    lo = (v - hi.astype(F32)).astype(BF16)
    return jnp.concatenate([hi, lo, hi], axis=0)


def exact_dot(a, b):
    return jnp.dot(a, b, precision=lax.Precision.HIGHEST, preferred_element_type=F32)


def widen(w):
    hi = w.astype(BF16)
    lo = (w - hi.astype(F32)).astype(BF16)
    return jnp.concatenate([hi, hi, lo], axis=1)


def kernel(ngx, ngy, src_h, kap_h, diag_h, faces_h, smooth_h, prol_h, both_out,
           src, kap, diag, faces, smooth, prol, s_in, q0, u1, u2, u3, q1, u11, u21, e1, q2, u12, u22, e2, pp, pb, rr,
           wm, wl, wb, wr, wp,
           s_q0, r_q0, s_qx, r_qx, s_qc, r_qc, s_u2b, r_u2b, s_g, r_g, s_rl, r_rl, s_q2, r_q2, s_u21, r_u21):
    sol, res = both_out.at[pl.ds(0, N * 8)], both_out.at[pl.ds(N * 8, N * 8)]
    gx, gy = lax.axis_index("gx"), lax.axis_index("gy")

    def inside(dx, dy):
        ok = None
        for at, d, n in ((gx, dx, ngx), (gy, dy, ngy)):
            if d:
                c = (at + d >= 0) & (at + d < n)
                ok = c if ok is None else ok & c
        return ok

    fetches = [pltpu.make_async_copy(a, b, s_in.at[i]) for i, (a, b) in enumerate((
        (src_h, src), (kap_h, kap), (smooth_h, smooth), (faces_h, faces), (diag_h, diag), (prol_h, prol)))]
    for f in fetches:
        f.start()

    barrier = pltpu.get_barrier_semaphore()
    partners = [(d, 0) for d in (-3, -2, -1, 1, 2, 3)] + [(0, d) for d in (-3, -2, -1, 1, 2, 3)]
    partners += [(a, b) for a in (-1, 1) for b in (-1, 1)]
    for dx, dy in partners:
        @pl.when(inside(dx, dy))
        def _():
            pl.semaphore_signal(barrier, inc=1, device_id=(gx + dx, gy + dy), device_id_type=MESH)
    fetches[1].wait()
    fetches[0].wait()
    for y in range(2):
        for x in range(4):
            c = x * 2 + y
            q0[2 + y, 2 + x] = src[pl.ds(c, N, stride=8), :] / kap[pl.ds(c, 1), :]
    peers = 0
    for dx, dy in partners:
        peers = peers + inside(dx, dy).astype(jnp.int32)
    pl.semaphore_wait(barrier, peers)

    def remote(s, d, ssem, rsem, dx, dy):
        return pltpu.make_async_remote_copy(
            src_ref=s, dst_ref=d, send_sem=ssem, recv_sem=rsem,
            device_id=(gx + dx, gy + dy), device_id_type=MESH)

    def send(s, d, ssem, rsem, dx, dy, cond=None):
        ok = inside(dx, dy) if cond is None else cond

        @pl.when(ok)
        def _():
            remote(s, d, ssem, rsem, dx, dy).start()

    def receive(d, ssem, rsem, dx, dy, cond=None):
        ok = inside(dx, dy) if cond is None else cond

        @pl.when(ok)
        def _():
            remote(d, d, ssem, rsem, dx, dy).wait_recv()

    def clear(ref, dx, dy):
        @pl.when(jnp.logical_not(inside(dx, dy)))
        def _():
            ref[...] = jnp.zeros(ref.shape, F32)

    def faces_x(buf):
        return [
            (buf.at[pl.ds(2, 2), 5], buf.at[pl.ds(2, 2), 1], 1, 0),
            (buf.at[pl.ds(2, 2), 2], buf.at[pl.ds(2, 2), 6], -1, 0),
            (buf.at[pl.ds(2, 2), 4], buf.at[pl.ds(2, 2), 0], 1, 0),
            (buf.at[pl.ds(2, 2), 3], buf.at[pl.ds(2, 2), 7], -1, 0),
        ]

    def near_y(buf, x, n):
        return [
            (buf.at[3, pl.ds(x, n)], buf.at[1, pl.ds(x, n)], 0, 1),
            (buf.at[2, pl.ds(x, n)], buf.at[4, pl.ds(x, n)], 0, -1),
        ]

    def far_y(buf, x, n):
        return [
            (buf.at[2, pl.ds(x, n)], buf.at[0, pl.ds(x, n)], 0, 1),
            (buf.at[3, pl.ds(x, n)], buf.at[5, pl.ds(x, n)], 0, -1),
        ]

    def corners(buf):
        return [
            (buf.at[3, 5], buf.at[1, 1], 1, 1),
            (buf.at[3, 2], buf.at[1, 6], -1, 1),
            (buf.at[2, 5], buf.at[4, 1], 1, -1),
            (buf.at[2, 2], buf.at[4, 6], -1, -1),
        ]

    def send_all(faces_of, ssem, rsem):
        for i, (s, d, dx, dy) in enumerate(faces_of):
            send(s, d, ssem.at[i], rsem.at[i], dx, dy)

    def receive_all(faces_of, ssem, rsem):
        for i, (s, d, dx, dy) in enumerate(faces_of):
            receive(d, ssem.at[i], rsem.at[i], -dx, -dy)

    q0_y = near_y(q0, 2, 1) + near_y(q0, 5, 1) + near_y(q0, 3, 2) + far_y(q0, 2, 2) + far_y(q0, 4, 2)
    q0_x = faces_x(q0)
    q0_c = [
        (q0.at[1, 5], q0.at[1, 1], 1, -1),
        (q0.at[4, 5], q0.at[4, 1], 1, 1),
        (q0.at[1, 2], q0.at[1, 6], -1, -1),
        (q0.at[4, 2], q0.at[4, 6], -1, 1),
    ]
    u2_more = far_y(u2, 2, 4) + faces_x(u2)[2:] + corners(u2)
    send_all(q0_y, s_q0, r_q0)
    send_all(q0_x, s_qx, r_qx)

    for f in fetches[2:]:
        f.wait()
    s8 = OMEGA * smooth[...]
    eye = (lax.broadcasted_iota(jnp.int32, (N, N), 0) == lax.broadcasted_iota(jnp.int32, (N, N), 1)).astype(F32)
    wm[pl.ds(SM, N), :] = widen(s8)
    for i, at in enumerate(FACES):
        f = faces[i]
        wb[pl.ds(at, N), :] = widen(-f)
        sf = exact_dot(s8, f)
        wl[pl.ds(at, N), :] = widen(sf)
        wm[pl.ds(at, N), :] = widen(exact_dot(sf, s8))
    d = diag[...]
    wb[pl.ds(CC, N), :] = widen(d)
    lc = eye - exact_dot(s8, d)
    wl[pl.ds(CC, N), :] = widen(lc)
    wm[pl.ds(CC, N), :] = widen(s8 + exact_dot(lc, s8))
    for i in range(4):
        p = prol[i]
        wp[pl.ds(N * i, N), :] = widen(p)
        wr[pl.ds(N * i, N), :] = widen(0.25 * p.T)

    for group in (q0_y, q0_x, u2_more):
        for _, dst, dx, dy in group:
            clear(dst, -dx, -dy)
    for _, dst, dx, dy in q0_c:
        clear(dst, -dx, dy)
    clear(q1.at[pl.ds(0, 2)], -1, 0)
    clear(q1.at[pl.ds(4, 2)], 1, 0)
    clear(u21.at[0], -1, 0)
    clear(u21.at[5], 1, 0)
    for dd in (1, 2, 3):
        clear(q2.at[3 - dd], -dd, 0)
        clear(q2.at[3 + dd], dd, 0)
    e1[:, 0] = jnp.zeros((4, N, LANES), F32)
    e1[:, 5] = jnp.zeros((4, N, LANES), F32)

    lane = lax.broadcasted_iota(jnp.int32, (N, LANES), 1)
    not_first, not_last = lane > 0, lane < LANES - 1

    def apply(w, row, rows, load, cols, at, to=pp):
        pair = jnp.concatenate([split(load(cols[0])), split(load(cols[1]))], axis=1)
        out = jnp.dot(w[pl.ds(row, rows), :], pair, preferred_element_type=F32)
        to[at[0], pl.ds(row, rows), :] = out[:, :LANES]
        to[at[1], pl.ds(row, rows), :] = out[:, LANES:]

    def gathered(c, sx, sy, ym=True, yp=True, of=pp):
        t = of[c, pl.ds(CC, N), :]
        t = t + of[c - sx, pl.ds(XM, N), :] + of[c + sx, pl.ds(XP, N), :]
        if ym:
            t = t + of[c - sy, pl.ds(YM, N), :]
        if yp:
            t = t + of[c + sy, pl.ds(YP, N), :]
        t = t + jnp.where(not_first, pltpu.roll(of[c, pl.ds(ZM, N), :], 1, 1), 0.0)
        t = t + jnp.where(not_last, pltpu.roll(of[c, pl.ds(ZP, N), :], LANES - 1, 1), 0.0)
        return t

    def loop(n, body):
        for i in range(n):
            body(i)

    def fine_at(y, x):
        return (y + 2) * 8 + x + 2

    def fine(w, row, rows, buf, c, e, to=pp):
        apply(w, row, rows, lambda p: buf[2 + p[0], 2 + p[1]], (c, e), (fine_at(*c), fine_at(*e)), to)

    def fine_own(w, rows, buf, to=pp):
        for y in range(2):
            for x in (0, 2):
                fine(w, 0, rows, buf, (y, x), (y, x + 1), to)

    def keep(ok):
        return jnp.where(ok, 1.0, 0.0).astype(F32)

    def present(offset):
        return keep((gx + offset >= 0) & (gx + offset < ngx))

    def side(offset):
        return keep((gy + offset >= 0) & (gy + offset < ngy))

    def take_u2(y, x, m=None):
        c = fine_at(y, x)
        v = gathered(c, 1, 8)
        u2[2 + y, 2 + x] = v if m is None else m * v
        u1[1 + y, 1 + x] = pp[c, pl.ds(SM, N), :]

    fine_own(wm, 512, q0)
    receive_all(q0_x, s_qx, r_qx)
    for y in range(2):
        fine(wm, 0, 512, q0, (y, -1), (y, 4))
        fine(wm, XM, 128, q0, (y, -2), (y, 5))

    def forward(group):
        for i, (s, d, dx, dy) in group:
            @pl.when(inside(dx, 0) & inside(0, dy))
            def _():
                pltpu.make_async_remote_copy(
                    src_ref=s, dst_ref=d, send_sem=s_qc.at[i], recv_sem=r_qc.at[i],
                    device_id=(gx + dx, gy), device_id_type=MESH).start()

    def receive_part(first, n):
        for i in range(first, first + n):
            s, d, dx, dy = q0_y[i]
            receive(d, s_q0.at[i], r_q0.at[i], -dx, -dy)

    receive_part(2, 2)
    forward([(0, q0_c[0]), (1, q0_c[1])])
    receive_part(0, 2)
    forward([(2, q0_c[2]), (3, q0_c[3])])
    receive_part(4, 2)
    for x in range(4):
        fine(wm, 0, 512, q0, (-1, x), (2, x))
    for y in range(2):
        for x in range(4):
            take_u2(y, x)
    fine_own(wb, 448, u2, pb)
    for i, (s, d, dx, dy) in enumerate(q0_c):
        @pl.when(inside(-dx, 0) & inside(0, dy))
        def _():
            pltpu.make_async_remote_copy(
                src_ref=d, dst_ref=d, send_sem=s_qc.at[i], recv_sem=r_qc.at[i],
                device_id=(gx - dx, gy), device_id_type=MESH).wait_recv()
    for y in (-1, 2):
        fine(wm, 0, 256, q0, (y, -1), (y, 4))
    for y in range(2):
        take_u2(y, -1, present(-1))
        take_u2(y, 4, present(1))
        fine(wb, XM, 128, u2, (y, -1), (y, 4), pb)

    def relay(j, at):
        for i, (dx, to) in enumerate(((1, 0), (-1, 4))):
            @pl.when(inside(dx, 0))
            def _():
                remote(q1.at[2 + at, j], q1.at[to + at, j], s_rl.at[i, at, j], r_rl.at[i, at, j], dx, 0).start()

    def half(at):
        receive_part(6 + 2 * at, 2)
        for x in (2 * at, 2 * at + 1):
            fine(wm, YM, 128, q0, (-2, x), (3, x))
        for x in (2 * at, 2 * at + 1):
            take_u2(-1, x, side(-1))
            take_u2(2, x, side(1))
        for x in (2 * at, 2 * at + 1):
            fine(wb, YM, 128, u2, (-1, x), (2, x), pb)
        total = None
        for x in (2 * at, 2 * at + 1):
            for y in range(2):
                t = gathered(fine_at(y, x), 1, 8, of=pb)
                k = kap[pl.ds(x * 2 + y, 1), :]
                r = split((q0[2 + y, 2 + x] - t) * k)
                child = 2 * (x - 2 * at) + y
                part = jnp.dot(wr[pl.ds(N * child, N), :], r, preferred_element_type=F32)
                total = part if total is None else total + part
        k1 = kap[pl.ds(4 * at, 1), :] + kap[pl.ds(4 * at + 1, 1), :]
        k1 = (k1 + (kap[pl.ds(4 * at + 2, 1), :] + kap[pl.ds(4 * at + 3, 1), :])) * 0.25
        q1[2 + at, gy, pl.ds(0, N), :] = total / k1
        q1[2 + at, gy, pl.ds(N, 8), :] = jnp.broadcast_to(k1, (8, LANES))
        for j in range(ngy):
            @pl.when(gy != j)
            def _():
                pltpu.make_async_remote_copy(
                    src_ref=q1.at[2 + at, gy], dst_ref=q1.at[2 + at, gy],
                    send_sem=s_g.at[at, j], recv_sem=r_g.at[at, gy],
                    device_id=(gx, j), device_id_type=MESH).start()
        relay(gy, at)

    half(0)
    half(1)

    def restrict(index):
        total = None
        for child in range(4):
            pair = jnp.concatenate([rr[index(0, child)], rr[index(1, child)]], axis=1)
            part = jnp.dot(wr[pl.ds(N * child, N), :], pair, preferred_element_type=F32)
            total = part if total is None else total + part
        return total[:, :LANES], total[:, LANES:]

    def arrive(j, at):
        block = q1.at[2 + at, j]
        pltpu.make_async_remote_copy(
            src_ref=block, dst_ref=block, send_sem=s_g.at[at, j], recv_sem=r_g.at[at, j],
            device_id=(gx, j), device_id_type=MESH).wait_recv()
        relay(j, at)
    for at in range(2):
        for dd in (1, -1, 2, -2, 3, -3):
            @pl.when(inside(0, dd))
            def _():
                arrive(gy + dd, at)
    send_all(u2_more, s_u2b, r_u2b)

    def coarse_own(w, rows, load, first, planes):
        def body(i):
            c = 4 * first + 2 * i
            apply(w, 0, rows, load, (c, c + 1), (c, c + 1))
        loop(2 * planes, body)

    def coarse_edges(w, load, low, high):
        def body(y):
            c, e = 4 * low + y, 4 * high + y
            apply(w, XM, 128, load, (c, e), (c, e))
        loop(4, body)

    def load_q1(c):
        return q1[c // 4, c % 4, pl.ds(0, N), :]

    def load_u21(c):
        return u21[c // 4, c % 4]

    coarse_own(wm, 512, load_q1, 2, 2)
    for at in range(2):
        for j in range(ngy):
            for i, (dx, to) in enumerate(((1, 0), (-1, 4))):
                @pl.when(inside(-dx, 0))
                def _():
                    block = q1.at[to + at, j]
                    remote(block, block, s_rl.at[i, at, j], r_rl.at[i, at, j], -dx, 0).wait_recv()
    coarse_own(wm, 512, load_q1, 1, 1)
    coarse_own(wm, 512, load_q1, 4, 1)
    coarse_edges(wm, load_q1, 0, 5)

    def device_of(x):
        return (x // 2) - 1

    def sum_u21(x):
        m = present(device_of(x))
        for y in range(4):
            c = 4 * x + y
            u21[x, y] = m * gathered(c, 4, 1, y > 0, y < 3)
            u11[x, y] = m * pp[c, pl.ds(SM, N), :]
    loop(4, lambda i: sum_u21(i + 1))

    u21_moves = [(u21.at[2], u21.at[0], 1, 0), (u21.at[3], u21.at[5], -1, 0)]
    send_all(u21_moves, s_u21, r_u21)
    coarse_own(wb, 448, load_u21, 2, 2)
    coarse_edges(wb, load_u21, 1, 4)

    def sum_r1(x):
        for y in range(4):
            t = gathered(4 * x + y, 4, 1, y > 0, y < 3)
            k1 = q1[x, y, pl.ds(N, 1), :]
            rr[(x - 2) * 4 + y] = split((q1[x, y, pl.ds(0, N), :] - t) * k1)
    loop(2, lambda i: sum_r1(i + 2))
    coarse2 = restrict(lambda at, child: (child // 2) * 4 + 2 * at + child % 2)
    for at in range(2):
        k2 = q1[2, 2 * at, pl.ds(N, 1), :] + q1[2, 2 * at + 1, pl.ds(N, 1), :]
        k2 = (k2 + (q1[3, 2 * at, pl.ds(N, 1), :] + q1[3, 2 * at + 1, pl.ds(N, 1), :])) * 0.25
        q2[3, at] = coarse2[at] / k2

    q2_moves = [(q2.at[3], q2.at[3 - dd], dd, 0) for dd in (1, -1, 2, -2, 3, -3)]
    send_all(q2_moves, s_q2, r_q2)

    def load_q2(c):
        return q2[c // 2, c % 2]

    def load_u22(c):
        return u22[c // 2, c % 2]

    def last_own(w, rows, load, first, planes):
        def body(i):
            c = 2 * first + 2 * i
            apply(w, 0, rows, load, (c, c + 1), (c, c + 1))
        loop(planes, body)

    def last_edges(w, load, low, high):
        def body(y):
            c, e = 2 * low + y, 2 * high + y
            apply(w, XM, 128, load, (c, e), (c, e))
        loop(2, body)

    last_own(wm, 512, load_q2, 3, 1)
    receive_all(q2_moves, s_q2, r_q2)
    last_own(wm, 512, load_q2, 1, 2)
    last_own(wm, 512, load_q2, 4, 2)
    last_edges(wm, load_q2, 0, 6)

    def sum_u22(x):
        m = present(x - 3)
        for y in range(2):
            u22[x, y] = m * gathered(2 * x + y, 2, 1, y > 0, y < 1)
            u12[x, y] = pp[2 * x + y, pl.ds(SM, N), :]
    loop(5, lambda i: sum_u22(i + 1))
    last_own(wl, 448, load_u22, 2, 3)
    last_edges(wl, load_u22, 1, 5)

    def sum_e2(x):
        m = present(x - 3)
        for y in range(2):
            e2[x - 2, y] = m * (u12[x, y] + gathered(2 * x + y, 2, 1, y > 0, y < 1))
    loop(3, lambda i: sum_e2(i + 2))

    receive_all(u21_moves, s_u21, r_u21)

    def prolong(load):
        pair = jnp.concatenate([split(load(0)), split(load(1))], axis=1)
        out = jnp.dot(wp[...], pair, preferred_element_type=F32)
        return lambda at, child: out[N * child:N * (child + 1), LANES * at:LANES * (at + 1)]

    for i, (s, dst, dx, dy) in enumerate(u21_moves):
        @pl.when(inside(dx, dy))
        def _():
            remote(s, dst, s_u21.at[i], r_u21.at[i], dx, dy).wait_send()

    def lift1(x2):
        part = prolong(lambda y: e2[x2, y])
        for y2 in range(2):
            for child in range(4):
                x, y = 2 * x2 + child // 2, 2 * y2 + child % 2
                u21[x, y] = u21[x, y] + part(y2, child)
    loop(3, lift1)
    coarse_own(wl, 448, load_u21, 1, 4)
    coarse_edges(wl, load_u21, 0, 5)

    def sum_e1(x):
        m = present(device_of(x))
        for y in range(4):
            e1[x - 1, 1 + y] = m * (u11[x, y] + gathered(4 * x + y, 4, 1, y > 0, y < 3))
    loop(4, lambda i: sum_e1(i + 1))

    receive_all(u2_more, s_u2b, r_u2b)
    for i, (s, dst, dx, dy) in enumerate(u2_more):
        @pl.when(inside(dx, dy))
        def _():
            remote(s, dst, s_u2b.at[i], r_u2b.at[i], dx, dy).wait_send()

    wanted = {(y, x) for y in range(-2, 4) for x in range(-2, 6)
              if max(0, -y, y - 1) + max(0, -x, x - 3) <= 2}
    for j in range(3):
        for xp in range(2):
            part = prolong(lambda i: e1[2 * xp + i, gy + j])
            for i in range(2):
                for child in range(4):
                    x = 2 * (2 * xp + i - 1) + child // 2
                    y = 2 * (j - 1) + child % 2
                    if (y, x) in wanted:
                        u2[2 + y, 2 + x] = u2[2 + y, 2 + x] + part(i, child)

    def load_u2(c):
        return u2[2 + c[0], 2 + c[1]]

    def both(w, row, rows, c, e):
        apply(w, row, rows, load_u2, (c, e), (fine_at(*c), fine_at(*e)))

    def rows_wide(i):
        y, x = i // 3, (i % 3) * 2 - 1
        both(wl, 0, 448, (y, x), (y, x + 1))
    loop(6, rows_wide)

    def rows_short(i):
        y, x = (i // 2) * 3 - 1, (i % 2) * 2
        both(wl, 0, 448, (y, x), (y, x + 1))
    loop(4, rows_short)
    loop(2, lambda y: both(wl, XM, 128, (y, -2), (y, 5)))
    loop(4, lambda x: both(wl, YM, 128, (-2, x), (3, x)))
    loop(2, lambda i: both(wl, 0, 256, (3 * i - 1, -1), (3 * i - 1, 4)))

    def sum_u3(y, x, m=None):
        v = u1[1 + y, 1 + x] + gathered(fine_at(y, x), 1, 8)
        u3[2 + y, 2 + x] = v if m is None else m * v
        return v

    def own_u3(i):
        y, x = i // 4, i % 4
        v = sum_u3(y, x)
        sol[pl.ds(x * 2 + y, N, stride=8), :] = v
    loop(8, own_u3)
    loop(2, lambda y: sum_u3(y, -1, present(-1)))
    loop(2, lambda y: sum_u3(y, 4, present(1)))
    loop(4, lambda x: sum_u3(-1, x, keep(gy > 0)))
    loop(4, lambda x: sum_u3(2, x, keep(gy < ngy - 1)))
    fine_own(wb, 448, u3)
    for y in range(2):
        fine(wb, XM, 128, u3, (y, -1), (y, 4))
    for x in range(4):
        fine(wb, YM, 128, u3, (-1, x), (2, x))

    def final(i):
        y, x = i // 4, i % 4
        c = x * 2 + y
        t = gathered(fine_at(y, x), 1, 8)
        res[pl.ds(c, N, stride=8), :] = src[pl.ds(c, N, stride=8), :] - kap[pl.ds(c, 1), :] * t
    loop(8, final)

    for group, ssem, rsem in ((q0_y, s_q0, r_q0), (q0_x, s_qx, r_qx), (q2_moves, s_q2, r_q2)):
        for i, (s, dst, dx, dy) in enumerate(group):
            @pl.when(inside(dx, dy))
            def _():
                remote(s, dst, ssem.at[i], rsem.at[i], dx, dy).wait_send()
    for i, (s, d, dx, dy) in enumerate(q0_c):
        @pl.when(inside(dx, 0) & inside(0, dy))
        def _():
            pltpu.make_async_remote_copy(
                src_ref=s, dst_ref=d, send_sem=s_qc.at[i], recv_sem=r_qc.at[i],
                device_id=(gx + dx, gy), device_id_type=MESH).wait_send()
    for at in range(2):
        for j in range(ngy):
            block = q1.at[2 + at, j]

            @pl.when(gy != j)
            def _():
                pltpu.make_async_remote_copy(
                    src_ref=block, dst_ref=block, send_sem=s_g.at[at, j], recv_sem=r_g.at[at, j],
                    device_id=(gx, j), device_id_type=MESH).wait_send()
            for i, (dx, to) in enumerate(((1, 0), (-1, 4))):
                @pl.when(inside(dx, 0))
                def _():
                    remote(block, q1.at[to + at, j], s_rl.at[i, at, j], r_rl.at[i, at, j], dx, 0).wait_send()


def solution(mesh):
    ngx, ngy = mesh.shape["gx"], mesh.shape["gy"]

    def shards(source, conductivity, diag_block, face_blocks, smoother, prolong):
        dma = pltpu.SemaphoreType.DMA
        col = (N, LANES)
        scratch = [
            pltpu.VMEM((N * 8, LANES), F32),
            pltpu.VMEM((8, LANES), F32),
            pltpu.VMEM((N, N), F32),
            pltpu.VMEM((6, N, N), F32),
            pltpu.VMEM((N, N), F32),
            pltpu.VMEM((4, N, N), F32),
            dma((6,)),
            pltpu.VMEM((6, 8) + col, F32),
            pltpu.VMEM((4, 6) + col, F32),
            pltpu.VMEM((6, 8) + col, F32),
            pltpu.VMEM((6, 8) + col, F32),
            pltpu.VMEM((6, 4, N + 8, LANES), F32),
            pltpu.VMEM((6, 4) + col, F32),
            pltpu.VMEM((6, 4) + col, F32),
            pltpu.VMEM((4, 6) + col, F32),
            pltpu.VMEM((7, 2) + col, F32),
            pltpu.VMEM((7, 2) + col, F32),
            pltpu.VMEM((7, 2) + col, F32),
            pltpu.VMEM((3, 2) + col, F32),
            pltpu.VMEM((48, 512, LANES), F32),
            pltpu.VMEM((48, 448, LANES), F32),
            pltpu.VMEM((8, 192, LANES), BF16),
            pltpu.VMEM((512, 192), BF16),
            pltpu.VMEM((448, 192), BF16),
            pltpu.VMEM((448, 192), BF16),
            pltpu.VMEM((256, 192), BF16),
            pltpu.VMEM((256, 192), BF16),
            dma((10,)), dma((10,)), dma((4,)), dma((4,)), dma((4,)), dma((4,)), dma((8,)), dma((8,)),
            dma((2, 4)), dma((2, 4)), dma((2, 2, 4)), dma((2, 2, 4)), dma((6,)), dma((6,)), dma((2,)), dma((2,)),
        ]
        shape = source.shape
        flat = jax.ShapeDtypeStruct((2 * N * 8, LANES), F32)
        vmem = pl.BlockSpec(memory_space=pltpu.VMEM)
        both = pl.pallas_call(
            functools.partial(kernel, ngx, ngy),
            out_shape=flat,
            in_specs=[pl.BlockSpec(memory_space=pl.ANY)] * 6,
            out_specs=vmem,
            scratch_shapes=scratch,
            compiler_params=pltpu.CompilerParams(
                collective_id=0, has_side_effects=True, vmem_limit_bytes=60 << 20),
            cost_estimate=pl.CostEstimate(flops=10**9, bytes_accessed=10**6, transcendentals=0),
        )(source.reshape(N * 8, LANES), conductivity.reshape(8, LANES),
          diag_block, face_blocks, smoother, prolong)
        return both[:N * 8].reshape(shape), both[N * 8:].reshape(shape)

    return jax.shard_map(
        shards,
        mesh=mesh,
        in_specs=(P(None, "gx", "gy", None), P("gx", "gy", None), P(), P(), P(), P()),
        out_specs=(P(None, "gx", "gy", None), P(None, "gx", "gy", None)),
        check_vma=False,
    )
```

time: 46.1 us -> 42.4 us (0.920)
  the two profiles are of different devices: /device:TPU:262 before, /device:TPU:241 now
where the time goes in v3:
time: 42.4 us; the launch traced here: 42.2 us
  Pallas kernels  39.7 us (94%)
  local copies, waits for them, and re-layouts  1.85 us (4%)
  between operations  0.64 us (2%)
    pallas_call x1, Pallas kernels, shards(): pl.pallas_call(functools.partial(kernel, ngx, ngy), out_shape=flat, in_sp...  39.7 us
    slice x1, local copies, waits for them, and re-layouts, shards(): return (both[:N * 8].reshape(shape), both[N * 8:].reshape(shape))  1.85 us

profile of v3, /device:TPU:241, one launch (start us, length us, event | category | flops | bytes accessed | tf_op | source)
XLA Modules:
  0.0 42.2 jit_solution(17344417461661765286)
XLA Ops:
  0.6 39.7 %shard_map.77 = f32[1024,128]{1,0:T(8,128)} custom-call(f32[512,128]{1,0:T(8,128)} %bitcast.6, f32[8,128]{1,0:T(8,128)} %bitcast.7, f32[64,64]{1,0:T(8,128)} %diag_h.1, f32[6,64,64]{2,1,0:T(8,128)} %faces_h.1, f32[64,64]{1,0:T(8,128)} %smooth_h.1, f32[4,64,64]{2,1,0:T(8,128)} %prol_h.1), custom_call_target="tpu_custom_call" | custom-call | flops 1000000000 | bytes 1000000 | tf_op jit(solution)/shard_map/pallas_call | solution.py:594
  40.4 1.9 %fusion = (f32[512,128]{1,0:T(8,128)}, f32[512,128]{1,0:T(8,128)}) fusion(f32[1024,128]{1,0:T(8,128)} %shard_map.77), kind=kLoop, calls=%fused_computation | loop fusion | bytes 1048576 | tf_op jit(solution)/shard_map/slice | solution.py:605

commit v4 on v3

--- a/solution.py
+++ b/solution.py
@@ -34,10 +34,14 @@
 
 
 def kernel(ngx, ngy, src_h, kap_h, diag_h, faces_h, smooth_h, prol_h, both_out,
-           src, kap, diag, faces, smooth, prol, s_in, q0, u1, u2, u3, q1, u11, u21, e1, q2, u12, u22, e2, pp, pb, rr,
+           held, s_out, src, kap, diag, faces, smooth, prol, s_in, q0, u1, u2, u3, q1, u11, u21, e1, q2, u12, u22, e2, pp, pb, rr,
            wm, wl, wb, wr, wp,
            s_q0, r_q0, s_qx, r_qx, s_qc, r_qc, s_u2b, r_u2b, s_g, r_g, s_rl, r_rl, s_q2, r_q2, s_u21, r_u21):
-    sol, res = both_out.at[pl.ds(0, N * 8)], both_out.at[pl.ds(N * 8, N * 8)]
+    sol, res = held.at[0], held.at[1]
+
+    def store(i):
+        return pltpu.make_async_copy(held.at[i], both_out.at[pl.ds(N * 8 * i, N * 8)], s_out.at[i])
+
     gx, gy = lax.axis_index("gx"), lax.axis_index("gy")
 
     def inside(dx, dy):
@@ -276,7 +280,7 @@
         for i, (dx, to) in enumerate(((1, 0), (-1, 4))):
             @pl.when(inside(dx, 0))
             def _():
-                remote(q1.at[2 + at, j], q1.at[to + at, j], s_rl.at[i, at, j], r_rl.at[i, at, j], dx, 0).start()
+                remote(q1.at[2 + at, j, pl.ds(0, N)], q1.at[to + at, j, pl.ds(0, N)], s_rl.at[i, at, j], r_rl.at[i, at, j], dx, 0).start()
 
     def half(at):
         receive_part(6 + 2 * at, 2)
@@ -357,7 +361,7 @@
             for i, (dx, to) in enumerate(((1, 0), (-1, 4))):
                 @pl.when(inside(-dx, 0))
                 def _():
-                    block = q1.at[to + at, j]
+                    block = q1.at[to + at, j, pl.ds(0, N)]
                     remote(block, block, s_rl.at[i, at, j], r_rl.at[i, at, j], -dx, 0).wait_recv()
     coarse_own(wm, 512, load_q1, 1, 1)
     coarse_own(wm, 512, load_q1, 4, 1)
@@ -374,7 +378,8 @@
             u11[x, y] = m * pp[c, pl.ds(SM, N), :]
     loop(4, lambda i: sum_u21(i + 1))
 
-    u21_moves = [(u21.at[2], u21.at[0], 1, 0), (u21.at[3], u21.at[5], -1, 0)]
+    low = pl.ds(jnp.clip(gy - 1, 0, ngy - 3), 3)
+    u21_moves = [(u21.at[2, low], u21.at[0, low], 1, 0), (u21.at[3, low], u21.at[5, low], -1, 0)]
     send_all(u21_moves, s_u21, r_u21)
     coarse_own(wb, 448, load_u21, 2, 2)
     coarse_edges(wb, load_u21, 1, 4)
@@ -413,6 +418,30 @@
         loop(2, body)
 
     last_own(wm, 512, load_q2, 3, 1)
+    for group, ssem, rsem in ((q0_y, s_q0, r_q0), (q0_x, s_qx, r_qx)):
+        for i, (s, dst, dx, dy) in enumerate(group):
+            @pl.when(inside(dx, dy))
+            def _():
+                remote(s, dst, ssem.at[i], rsem.at[i], dx, dy).wait_send()
+    for i, (s, d, dx, dy) in enumerate(q0_c):
+        @pl.when(inside(dx, 0) & inside(0, dy))
+        def _():
+            pltpu.make_async_remote_copy(
+                src_ref=s, dst_ref=d, send_sem=s_qc.at[i], recv_sem=r_qc.at[i],
+                device_id=(gx + dx, gy), device_id_type=MESH).wait_send()
+    for at in range(2):
+        for j in range(ngy):
+            block = q1.at[2 + at, j]
+
+            @pl.when(gy != j)
+            def _():
+                pltpu.make_async_remote_copy(
+                    src_ref=block, dst_ref=block, send_sem=s_g.at[at, j], recv_sem=r_g.at[at, j],
+                    device_id=(gx, j), device_id_type=MESH).wait_send()
+            for i, (dx, to) in enumerate(((1, 0), (-1, 4))):
+                @pl.when(inside(dx, 0))
+                def _():
+                    remote(block.at[pl.ds(0, N)], q1.at[to + at, j, pl.ds(0, N)], s_rl.at[i, at, j], r_rl.at[i, at, j], dx, 0).wait_send()
     receive_all(q2_moves, s_q2, r_q2)
     last_own(wm, 512, load_q2, 1, 2)
     last_own(wm, 512, load_q2, 4, 2)
@@ -439,6 +468,11 @@
         pair = jnp.concatenate([split(load(0)), split(load(1))], axis=1)
         out = jnp.dot(wp[...], pair, preferred_element_type=F32)
         return lambda at, child: out[N * child:N * (child + 1), LANES * at:LANES * (at + 1)]
+
+    for i, (s, dst, dx, dy) in enumerate(q2_moves):
+        @pl.when(inside(dx, dy))
+        def _():
+            remote(s, dst, s_q2.at[i], r_q2.at[i], dx, dy).wait_send()
 
     for i, (s, dst, dx, dy) in enumerate(u21_moves):
         @pl.when(inside(dx, dy))
@@ -508,6 +542,7 @@
         v = sum_u3(y, x)
         sol[pl.ds(x * 2 + y, N, stride=8), :] = v
     loop(8, own_u3)
+    store(0).start()
     loop(2, lambda y: sum_u3(y, -1, present(-1)))
     loop(2, lambda y: sum_u3(y, 4, present(1)))
     loop(4, lambda x: sum_u3(-1, x, keep(gy > 0)))
@@ -524,31 +559,10 @@
         t = gathered(fine_at(y, x), 1, 8)
         res[pl.ds(c, N, stride=8), :] = src[pl.ds(c, N, stride=8), :] - kap[pl.ds(c, 1), :] * t
     loop(8, final)
-
-    for group, ssem, rsem in ((q0_y, s_q0, r_q0), (q0_x, s_qx, r_qx), (q2_moves, s_q2, r_q2)):
-        for i, (s, dst, dx, dy) in enumerate(group):
-            @pl.when(inside(dx, dy))
-            def _():
-                remote(s, dst, ssem.at[i], rsem.at[i], dx, dy).wait_send()
-    for i, (s, d, dx, dy) in enumerate(q0_c):
-        @pl.when(inside(dx, 0) & inside(0, dy))
-        def _():
-            pltpu.make_async_remote_copy(
-                src_ref=s, dst_ref=d, send_sem=s_qc.at[i], recv_sem=r_qc.at[i],
-                device_id=(gx + dx, gy), device_id_type=MESH).wait_send()
-    for at in range(2):
-        for j in range(ngy):
-            block = q1.at[2 + at, j]
-
-            @pl.when(gy != j)
-            def _():
-                pltpu.make_async_remote_copy(
-                    src_ref=block, dst_ref=block, send_sem=s_g.at[at, j], recv_sem=r_g.at[at, j],
-                    device_id=(gx, j), device_id_type=MESH).wait_send()
-            for i, (dx, to) in enumerate(((1, 0), (-1, 4))):
-                @pl.when(inside(dx, 0))
-                def _():
-                    remote(block, q1.at[to + at, j], s_rl.at[i, at, j], r_rl.at[i, at, j], dx, 0).wait_send()
+    store(1).start()
+
+    store(0).wait()
+    store(1).wait()
 
 
 def solution(mesh):
@@ -558,6 +572,8 @@
         dma = pltpu.SemaphoreType.DMA
         col = (N, LANES)
         scratch = [
+            pltpu.VMEM((2, N * 8, LANES), F32),
+            dma((2,)),
             pltpu.VMEM((N * 8, LANES), F32),
             pltpu.VMEM((8, LANES), F32),
             pltpu.VMEM((N, N), F32),
@@ -590,12 +606,11 @@
         ]
         shape = source.shape
         flat = jax.ShapeDtypeStruct((2 * N * 8, LANES), F32)
-        vmem = pl.BlockSpec(memory_space=pltpu.VMEM)
         both = pl.pallas_call(
             functools.partial(kernel, ngx, ngy),
             out_shape=flat,
             in_specs=[pl.BlockSpec(memory_space=pl.ANY)] * 6,
-            out_specs=vmem,
+            out_specs=pl.BlockSpec(memory_space=pl.ANY),
             scratch_shapes=scratch,
             compiler_params=pltpu.CompilerParams(
                 collective_id=0, has_side_effects=True, vmem_limit_bytes=60 << 20),

time: 42.4 us -> 41.7 us (0.983)
  Pallas kernels: 39.7 us -> 39.1 us
    pallas_call x1, Pallas kernels: 39.7 us -> 39.1 us  [shards(): pl.pallas_call(functools.partial(kernel, ngx, ngy), out_shape=flat, in_sp...]
where the time goes in v4:
time: 41.7 us; the launch traced here: 41.6 us
  Pallas kernels  39.1 us (94%)
  local copies, waits for them, and re-layouts  1.85 us (4%)
  between operations  0.64 us (2%)
    pallas_call x1, Pallas kernels, shards(): pl.pallas_call(functools.partial(kernel, ngx, ngy), out_shape=flat, in_sp...  39.1 us
    slice x1, local copies, waits for them, and re-layouts, shards(): return (both[:N * 8].reshape(shape), both[N * 8:].reshape(shape))  1.85 us

profile of v4, /device:TPU:241, one launch (start us, length us, event | category | flops | bytes accessed | tf_op | source)
XLA Modules:
  0.0 41.6 jit_solution(8793743426830906542)
XLA Ops:
  0.6 39.1 %shard_map.77 = f32[1024,128]{1,0:T(8,128)} custom-call(f32[512,128]{1,0:T(8,128)} %bitcast.6, f32[8,128]{1,0:T(8,128)} %bitcast.7, f32[64,64]{1,0:T(8,128)} %diag_h.1, f32[6,64,64]{2,1,0:T(8,128)} %faces_h.1, f32[64,64]{1,0:T(8,128)} %smooth_h.1, f32[4,64,64]{2,1,0:T(8,128)} %prol_h.1), custom_call_target="tpu_custom_call" | custom-call | flops 1000000000 | bytes 1000000 | tf_op jit(solution)/shard_map/pallas_call | solution.py:609
  39.7 1.9 %fusion = (f32[512,128]{1,0:T(8,128)}, f32[512,128]{1,0:T(8,128)}) fusion(f32[1024,128]{1,0:T(8,128)} %shard_map.77), kind=kLoop, calls=%fused_computation | loop fusion | bytes 1048576 | tf_op jit(solution)/shard_map/slice | solution.py:620

commit v5 on v4

--- a/solution.py
+++ b/solution.py
@@ -363,8 +363,7 @@
                 def _():
                     block = q1.at[to + at, j, pl.ds(0, N)]
                     remote(block, block, s_rl.at[i, at, j], r_rl.at[i, at, j], -dx, 0).wait_recv()
-    coarse_own(wm, 512, load_q1, 1, 1)
-    coarse_own(wm, 512, load_q1, 4, 1)
+        coarse_own(wm, 512, load_q1, 1 if at else 4, 1)
     coarse_edges(wm, load_q1, 0, 5)
 
     def device_of(x):
@@ -396,7 +395,7 @@
         k2 = (k2 + (q1[3, 2 * at, pl.ds(N, 1), :] + q1[3, 2 * at + 1, pl.ds(N, 1), :])) * 0.25
         q2[3, at] = coarse2[at] / k2
 
-    q2_moves = [(q2.at[3], q2.at[3 - dd], dd, 0) for dd in (1, -1, 2, -2, 3, -3)]
+    q2_moves = [(q2.at[3], q2.at[3 - dd], dd, 0) for dd in (3, -3, 2, -2, 1, -1)]
     send_all(q2_moves, s_q2, r_q2)
 
     def load_q2(c):
@@ -442,9 +441,18 @@
                 @pl.when(inside(dx, 0))
                 def _():
                     remote(block.at[pl.ds(0, N)], q1.at[to + at, j, pl.ds(0, N)], s_rl.at[i, at, j], r_rl.at[i, at, j], dx, 0).wait_send()
-    receive_all(q2_moves, s_q2, r_q2)
-    last_own(wm, 512, load_q2, 1, 2)
-    last_own(wm, 512, load_q2, 4, 2)
+    def receive_q2(distance):
+        for i, (s, d, dx, dy) in enumerate(q2_moves):
+            if abs(dx) == distance:
+                receive(d, s_q2.at[i], r_q2.at[i], -dx, -dy)
+
+    receive_q2(1)
+    last_own(wm, 512, load_q2, 2, 1)
+    last_own(wm, 512, load_q2, 4, 1)
+    receive_q2(2)
+    last_own(wm, 512, load_q2, 1, 1)
+    last_own(wm, 512, load_q2, 5, 1)
+    receive_q2(3)
     last_edges(wm, load_q2, 0, 6)
 
     def sum_u22(x):

time: 41.7 us -> 42 us (level)
  the two profiles are of different devices: /device:TPU:241 before, /device:TPU:256 now
where the time goes in v5:
time: 42 us; the launch traced here: 41.8 us
  Pallas kernels  39.3 us (94%)
  local copies, waits for them, and re-layouts  1.85 us (4%)
  between operations  0.64 us (2%)
    pallas_call x1, Pallas kernels, shards(): pl.pallas_call(functools.partial(kernel, ngx, ngy), out_shape=flat, in_sp...  39.3 us
    slice x1, local copies, waits for them, and re-layouts, shards(): return (both[:N * 8].reshape(shape), both[N * 8:].reshape(shape))  1.85 us

profile of v5, /device:TPU:256, one launch (start us, length us, event | category | flops | bytes accessed | tf_op | source)
XLA Modules:
  0.0 41.8 jit_solution(7711830264392444885)
XLA Ops:
  0.6 39.3 %shard_map.77 = f32[1024,128]{1,0:T(8,128)} custom-call(f32[512,128]{1,0:T(8,128)} %bitcast.6, f32[8,128]{1,0:T(8,128)} %bitcast.7, f32[64,64]{1,0:T(8,128)} %diag_h.1, f32[6,64,64]{2,1,0:T(8,128)} %faces_h.1, f32[64,64]{1,0:T(8,128)} %smooth_h.1, f32[4,64,64]{2,1,0:T(8,128)} %prol_h.1), custom_call_target="tpu_custom_call" | custom-call | flops 1000000000 | bytes 1000000 | tf_op jit(solution)/shard_map/pallas_call | solution.py:617
  40.0 1.9 %fusion = (f32[512,128]{1,0:T(8,128)}, f32[512,128]{1,0:T(8,128)}) fusion(f32[1024,128]{1,0:T(8,128)} %shard_map.77), kind=kLoop, calls=%fused_computation | loop fusion | bytes 1048576 | tf_op jit(solution)/shard_map/slice | solution.py:628

commit v6 on v5

--- a/solution.py
+++ b/solution.py
@@ -379,7 +379,6 @@
 
     low = pl.ds(jnp.clip(gy - 1, 0, ngy - 3), 3)
     u21_moves = [(u21.at[2, low], u21.at[0, low], 1, 0), (u21.at[3, low], u21.at[5, low], -1, 0)]
-    send_all(u21_moves, s_u21, r_u21)
     coarse_own(wb, 448, load_u21, 2, 2)
     coarse_edges(wb, load_u21, 1, 4)
 
@@ -397,6 +396,7 @@
 
     q2_moves = [(q2.at[3], q2.at[3 - dd], dd, 0) for dd in (3, -3, 2, -2, 1, -1)]
     send_all(q2_moves, s_q2, r_q2)
+    send_all(u21_moves, s_u21, r_u21)
 
     def load_q2(c):
         return q2[c // 2, c % 2]

time: 42 us -> 41.9 us (level)
  no operation moved by 1% of the time
where the time goes in v6:
time: 41.9 us; the launch traced here: 41.7 us
  Pallas kernels  39.3 us (94%)
  local copies, waits for them, and re-layouts  1.85 us (4%)
  between operations  0.64 us (2%)
    pallas_call x1, Pallas kernels, shards(): pl.pallas_call(functools.partial(kernel, ngx, ngy), out_shape=flat, in_sp...  39.3 us
    slice x1, local copies, waits for them, and re-layouts, shards(): return (both[:N * 8].reshape(shape), both[N * 8:].reshape(shape))  1.85 us

profile of v6, /device:TPU:256, one launch (start us, length us, event | category | flops | bytes accessed | tf_op | source)
XLA Modules:
  0.0 41.7 jit_solution(3403256949982699827)
XLA Ops:
  0.6 39.3 %shard_map.77 = f32[1024,128]{1,0:T(8,128)} custom-call(f32[512,128]{1,0:T(8,128)} %bitcast.6, f32[8,128]{1,0:T(8,128)} %bitcast.7, f32[64,64]{1,0:T(8,128)} %diag_h.1, f32[6,64,64]{2,1,0:T(8,128)} %faces_h.1, f32[64,64]{1,0:T(8,128)} %smooth_h.1, f32[4,64,64]{2,1,0:T(8,128)} %prol_h.1), custom_call_target="tpu_custom_call" | custom-call | flops 1000000000 | bytes 1000000 | tf_op jit(solution)/shard_map/pallas_call | solution.py:617
  39.9 1.9 %fusion = (f32[512,128]{1,0:T(8,128)}, f32[512,128]{1,0:T(8,128)}) fusion(f32[1024,128]{1,0:T(8,128)} %shard_map.77), kind=kLoop, calls=%fused_computation | loop fusion | bytes 1048576 | tf_op jit(solution)/shard_map/slice | solution.py:628

commit v7 on v6

--- a/solution.py
+++ b/solution.py
@@ -394,7 +394,7 @@
         k2 = (k2 + (q1[3, 2 * at, pl.ds(N, 1), :] + q1[3, 2 * at + 1, pl.ds(N, 1), :])) * 0.25
         q2[3, at] = coarse2[at] / k2
 
-    q2_moves = [(q2.at[3], q2.at[3 - dd], dd, 0) for dd in (3, -3, 2, -2, 1, -1)]
+    q2_moves = [(q2.at[3], q2.at[3 - dd], dd, 0) for dd in (1, -1, 2, -2, 3, -3)]
     send_all(q2_moves, s_q2, r_q2)
     send_all(u21_moves, s_u21, r_u21)
 

time: 41.9 us -> 40.9 us (0.976)
  the two profiles are of different devices: /device:TPU:256 before, /device:TPU:249 now
where the time goes in v7:
time: 40.9 us; the launch traced here: 40.8 us
  Pallas kernels  38.3 us (94%)
  local copies, waits for them, and re-layouts  1.85 us (5%)
  between operations  0.64 us (2%)
    pallas_call x1, Pallas kernels, shards(): pl.pallas_call(functools.partial(kernel, ngx, ngy), out_shape=flat, in_sp...  38.3 us
    slice x1, local copies, waits for them, and re-layouts, shards(): return (both[:N * 8].reshape(shape), both[N * 8:].reshape(shape))  1.85 us

profile of v7, /device:TPU:249, one launch (start us, length us, event | category | flops | bytes accessed | tf_op | source)
XLA Modules:
  0.0 40.8 jit_solution(8099373962151051023)
XLA Ops:
  0.6 38.3 %shard_map.77 = f32[1024,128]{1,0:T(8,128)} custom-call(f32[512,128]{1,0:T(8,128)} %bitcast.6, f32[8,128]{1,0:T(8,128)} %bitcast.7, f32[64,64]{1,0:T(8,128)} %diag_h.1, f32[6,64,64]{2,1,0:T(8,128)} %faces_h.1, f32[64,64]{1,0:T(8,128)} %smooth_h.1, f32[4,64,64]{2,1,0:T(8,128)} %prol_h.1), custom_call_target="tpu_custom_call" | custom-call | flops 1000000000 | bytes 1000000 | tf_op jit(solution)/shard_map/pallas_call | solution.py:617
  38.9 1.9 %fusion = (f32[512,128]{1,0:T(8,128)}, f32[512,128]{1,0:T(8,128)}) fusion(f32[1024,128]{1,0:T(8,128)} %shard_map.77), kind=kLoop, calls=%fused_computation | loop fusion | bytes 1048576 | tf_op jit(solution)/shard_map/slice | solution.py:628
